TPU v7x, 32 devices: a whole 2x2x4 slice. The times are simulated.
32 devices in a mesh: ctx: 4 (over y, x), head: 8 (over z, core).
Axes of the slice: x: 2, y: 2, z: 4, core: 2. Of those that a mesh axis runs over, the one named last changes fastest.
Arguments:
- doc_lengths: int32 [4], replicated, may hold values from 1 to 1536, 2048 in all
- lin_q: bfloat16 [2048, 8192], P('ctx', 'head'), may hold values from -6 to 6
- lin_k: bfloat16 [2048, 8192], P('ctx', 'head'), may hold values from -6 to 6
- lin_v: bfloat16 [2048, 8192], P('ctx', 'head'), may hold values from -40 to 40
- log_decay: float32 [64, 2048], P('head', 'ctx'), may hold values from -1 to 0
- lin_gain: float32 [8192], P('head'), may hold values from 0.5 to 1.5
- soft_q: bfloat16 [2048, 8192], P('ctx', 'head'), may hold values from -48 to 48
- soft_k: bfloat16 [2048, 1024], P('ctx', 'head'), may hold values from -6 to 6
- soft_v: bfloat16 [2048, 1024], P('ctx', 'head'), may hold values from -6 to 6
Outputs:
- lin_out: bfloat16 [2048, 8192], P('ctx', 'head')
- soft_out: bfloat16 [2048, 8192], P('ctx', 'head')
Inputs may be any that keep to these rules, and one draw needn't show every extreme that they name: `doc_lengths`: the 4 lengths sum to 2048 and the largest is exactly 1536.
All inputs are finite; a program needn't handle non-finite values.
Results may differ from a plain program's by a relative error of at most 0.015.
Values may be sent and summed in bfloat16 or wider, within the bound.
No kernel may reach another device: no remote copies, remote signals or barrier semaphores. Data moves between devices by JAX's collectives and lax.ppermute only.
A program may use at most 64 MiB of HBM per device.

v0:
```python
import functools

import jax
import jax.numpy as jnp
from jax import lax
from jax.experimental import pallas as pl
from jax.experimental.pallas import tpu as pltpu
from jax.sharding import PartitionSpec as P

KVH = 8
DH = 128
BLK = 256
ROWS = 256
PLACED = 90.0
LOW = -1e30
LOG2E = 1.4426950408889634
FACTOR = LOG2E * DH**-0.5
F32 = jnp.float32
BF16 = jnp.bfloat16
NT = (((1,), (1,)), ((), ()))
TN = (((0,), (0,)), ((), ()))
HBM = pl.BlockSpec(memory_space=pltpu.HBM)
VMEM = pl.BlockSpec(memory_space=pltpu.VMEM)


def within(mib):
    return pltpu.CompilerParams(vmem_limit_bytes=mib * 1024 * 1024)


def lasting(us):
    return pl.CostEstimate(flops=int(us * 0.8e9), bytes_accessed=0, transcendentals=0)


def swapped(value, axis, bit):
    return lax.ppermute(value, axis, [(i, i ^ 1 << bit) for i in range(lax.axis_size(axis))])


def bounds_of(lengths_ref):
    out, total = [], 0
    lengths = lengths_ref[...]
    for d in range(lengths.shape[1]):
        total = total + lengths[0, d]
        out.append(total)
    return out


def doc_start(bounds, position):
    start = jnp.zeros_like(position)
    for bound in bounds:
        start = jnp.where(bound <= position, bound, start)
    return start


def log_sums(decay):
    rows = lax.broadcasted_iota(jnp.int32, (BLK, BLK), 0)
    cols = lax.broadcasted_iota(jnp.int32, (BLK, BLK), 1)
    upper = jnp.where(rows <= cols, 1.0, 0.0).astype(BF16)
    found = jnp.dot(split(decay, 3).astype(BF16), upper, preferred_element_type=F32)
    count = decay.shape[0]
    return found[:count] + found[count : 2 * count] + found[2 * count :]


def split(value, count):
    terms = []
    for _ in range(count):
        term = value.astype(BF16).astype(F32)
        terms.append(term)
        value = value - term
    return jnp.concatenate(terms, axis=0)


def over_lanes(rows_form, count):
    heads = rows_form.shape[0]
    stacked = split(rows_form, count)
    extra = -stacked.shape[0] % 16
    if extra:
        stacked = jnp.concatenate([stacked, jnp.zeros((extra, stacked.shape[1]), F32)], axis=0)
    depth = stacked.shape[0]
    row = lax.broadcasted_iota(jnp.int32, (depth, heads * DH), 0)
    col = lax.broadcasted_iota(jnp.int32, (depth, heads * DH), 1)
    picks = jnp.where((row % heads == col // DH) & (row < count * heads), 1.0, 0.0).astype(BF16)
    return lax.dot_general(stacked.astype(BF16), picks, TN, preferred_element_type=F32)


def states_kernel(lengths_ref, keys_hbm, values_hbm, decay_ref, msg_ref, first_ref, sums_ref, keys_ref, values_ref, sems):
    heads = decay_ref.shape[0]
    tokens = keys_ref.shape[0]
    base = lax.axis_index("ctx") * tokens
    bounds = bounds_of(lengths_ref)
    place = lax.broadcasted_iota(jnp.int32, (1, BLK), 1)
    blocks = tokens // BLK
    copies = []
    for b in range(blocks):
        rows = slice(b * BLK, (b + 1) * BLK)
        copies.append(pltpu.make_async_copy(keys_hbm.at[rows, :], keys_ref.at[rows, :], sems.at[0, b]))
        copies.append(pltpu.make_async_copy(values_hbm.at[rows, :], values_ref.at[rows, :], sems.at[1, b]))
    for copy in copies:
        copy.start()
    through = jnp.ones((heads, 1), F32)
    weights, factors = [], []
    for b in range(blocks):
        s = base + b * BLK
        start_last = doc_start(bounds, s + BLK - 1)
        kept = jnp.where(start_last < s, 1.0, 0.0).astype(F32)
        sums = log_sums(decay_ref[:, b * BLK : (b + 1) * BLK])
        sums_ref[:, b * BLK : (b + 1) * BLK] = sums
        closing = sums[:, BLK - 1 : BLK]
        weight = jnp.where(s + place >= start_last, jnp.exp(closing - sums), 0.0)
        weights.append(over_lanes(weight, 2))
        factors.append(kept * jnp.exp(closing))
        through = through * factors[b]
    state = [None] * heads
    for b in range(blocks):
        copies[2 * b].wait()
        copies[2 * b + 1].wait()
        rows = slice(b * BLK, (b + 1) * BLK)
        for h in range(heads):
            cols = slice(h * DH, (h + 1) * DH)
            weighted = (keys_ref[rows, cols].astype(F32) * weights[b][:, cols]).astype(BF16)
            update = lax.dot_general(weighted, values_ref[rows, cols], TN, preferred_element_type=F32)
            state[h] = update if b == 0 else factors[b][h : h + 1, :] * state[h] + update
            if b < blocks - 1:
                first_ref[b, cols, :] = update.astype(BF16)
    for h in range(heads):
        msg_ref[h * DH : (h + 1) * DH, :] = state[h].astype(BF16)
    tail = jnp.broadcast_to(split(through, 2), (2 * heads, DH))
    extra = msg_ref.shape[0] - heads * DH - 2 * heads
    if extra:
        tail = jnp.concatenate([tail, jnp.zeros((extra, DH), F32)], axis=0)
    msg_ref[heads * DH :, :] = tail.astype(BF16)


def inside_kernel(lengths_ref, queries_ref, keys_ref, values_ref, sums_ref, out_ref):
    heads = sums_ref.shape[0]
    tokens = keys_ref.shape[0]
    base = lax.axis_index("ctx") * tokens
    bounds = bounds_of(lengths_ref)
    rows = lax.broadcasted_iota(jnp.int32, (BLK, BLK), 0)
    cols = lax.broadcasted_iota(jnp.int32, (BLK, BLK), 1)
    place = lax.broadcasted_iota(jnp.int32, (BLK, 1), 0)
    for b in range(tokens // BLK):
        s = base + b * BLK
        start = doc_start(bounds, s + place) - s
        bias = jnp.where((cols <= rows) & (cols >= start), 0.0, LOW)
        here = slice(b * BLK, (b + 1) * BLK)
        sums = sums_ref[:, here] * LOG2E
        down = over_lanes(sums, 3)
        for h in range(heads):
            there = slice(h * DH, (h + 1) * DH)
            upright = jnp.concatenate([down[:, there]] * (BLK // DH), axis=1)
            spread = upright - sums[h : h + 1, :] + bias
            scores = lax.dot_general(
                queries_ref[here, there], keys_ref[here, there], NT, preferred_element_type=F32
            )
            scores = (scores * jnp.exp2(spread)).astype(BF16)
            out_ref[here, there] = jnp.dot(
                scores, values_ref[here, there], preferred_element_type=F32
            ).astype(BF16)


def through_of(msg_ref, heads, h):
    high = msg_ref[heads * DH + h : heads * DH + h + 1, :].astype(F32)
    low = msg_ref[heads * DH + heads + h : heads * DH + heads + h + 1, :].astype(F32)
    return high + low


def joined(heads, early_ref, late_ref, swap, out_ref):
    def pick(here):
        one, two = early_ref[here, :].astype(F32), late_ref[here, :].astype(F32)
        return jnp.where(swap, two, one), jnp.where(swap, one, two)

    def through(h):
        high = pick(slice(heads * DH + h, heads * DH + h + 1))
        low = pick(slice(heads * DH + heads + h, heads * DH + heads + h + 1))
        return high[0] + low[0], high[1] + low[1]

    tails = []
    for h in range(heads):
        here = slice(h * DH, (h + 1) * DH)
        early, late = pick(here)
        early_through, late_through = through(h)
        out_ref[here, :] = (late_through * early + late).astype(BF16)
        tails.append(late_through * early_through)
    tail = jnp.concatenate(tails, axis=0)
    high = tail.astype(BF16).astype(F32)
    pieces = [high, tail - high]
    extra = out_ref.shape[0] - heads * DH - 2 * heads
    if extra:
        pieces.append(jnp.zeros((extra, DH), F32))
    out_ref[heads * DH :, :] = jnp.concatenate(pieces, axis=0).astype(BF16)


def upper_half(bit):
    return (lax.axis_index("ctx") // (1 << bit)) % 2 == 1


def total_kernel(heads, bit, total_ref, far_ref, new_total_ref):
    joined(heads, total_ref, far_ref, upper_half(bit), new_total_ref)


def prefix_kernel(heads, bit, prefix_ref, far_ref, new_prefix_ref):
    if bit == 1:
        first = jnp.where(upper_half(0), 1.0, 0.0).astype(F32)
        rows = prefix_ref.shape[0]
        tail = lax.broadcasted_iota(jnp.int32, (rows, DH), 0) - heads * DH
        own = prefix_ref[...].astype(F32) * first
        neutral = jnp.where((tail >= 0) & (tail < heads), 1.0 - first, 0.0)
        prefix_ref = (own + neutral).astype(BF16)

    @pl.when(upper_half(bit))
    def _():
        joined(heads, far_ref, prefix_ref, False, new_prefix_ref)

    @pl.when(jnp.logical_not(upper_half(bit)))
    def _():
        new_prefix_ref[...] = prefix_ref[...]


def across_kernel(
    bit, lengths_ref, queries_ref, inside_ref, sums_ref, gain_ref, first_ref, prefix_ref, far_ref, soft_ref,
    out_hbm, soft_hbm, out_ref, sems,
):
    soft_copy = pltpu.make_async_copy(soft_ref, soft_hbm, sems.at[0])
    soft_copy.start()
    copies = []
    heads = sums_ref.shape[0]
    tokens = queries_ref.shape[0]
    place_ctx = lax.axis_index("ctx")
    base = place_ctx * tokens
    upper = jnp.where(upper_half(bit), 1.0, 0.0).astype(F32)
    valid = jnp.where(upper_half(0), 1.0, 0.0).astype(F32) if bit == 1 else 1.0
    bounds = bounds_of(lengths_ref)
    place = lax.broadcasted_iota(jnp.int32, (1, BLK), 1)
    state = []
    for h in range(heads):
        here = slice(h * DH, (h + 1) * DH)
        through = upper * (valid * through_of(prefix_ref, heads, h) + (1.0 - valid))
        state.append(valid * prefix_ref[here, :].astype(F32) + through * far_ref[here, :].astype(F32))
    ones = jnp.ones((DH, DH), BF16)
    for b in range(tokens // BLK):
        s = base + b * BLK
        here = slice(b * BLK, (b + 1) * BLK)
        start_last = doc_start(bounds, s + BLK - 1)
        kept = jnp.where(start_last < s, 1.0, 0.0).astype(F32)
        sums = sums_ref[:, here]
        factor = kept * jnp.exp(sums[:, BLK - 1 : BLK])
        entering = jnp.where(doc_start(bounds, s + place) < s, jnp.exp(sums), 0.0)
        entering = over_lanes(entering, 2)
        for h in range(heads):
            there = slice(h * DH, (h + 1) * DH)
            across = jnp.dot(queries_ref[here, there], state[h].astype(BF16), preferred_element_type=F32)
            raw = inside_ref[here, there].astype(F32) + across * entering[:, there]
            square = jnp.dot((raw * raw).astype(BF16), ones, preferred_element_type=F32)
            scale = lax.rsqrt(square * (1.0 / DH) + 1e-06)
            out_ref[here, there] = (raw * scale * gain_ref[:, there]).astype(BF16)
            if b < tokens // BLK - 1:
                state[h] = factor[h : h + 1, :] * state[h] + first_ref[b, there, :].astype(F32)
        copies.append(pltpu.make_async_copy(out_ref.at[here, :], out_hbm.at[here, :], sems.at[1 + b]))
        copies[b].start()
    soft_copy.wait()
    for copy in copies:
        copy.wait()


def origin_of(m, count):
    place = lax.axis_index("ctx")
    origin = jnp.int32(0)
    bit = 1
    while bit < count:
        mine = (place // bit) % 2
        origin = origin + bit * (1 - mine if m & bit else mine)
        bit *= 2
    return origin


def bias_of(bounds, first_row, rows, first_key, count):
    row = first_row + lax.broadcasted_iota(jnp.int32, (rows, 1), 0)
    key = first_key + lax.broadcasted_iota(jnp.int32, (rows, count), 1)
    return jnp.where((key >= doc_start(bounds, row)) & (key <= row), 0.0, LOW)


def with_ones(values):
    return jnp.concatenate([values, jnp.ones(values.shape, BF16)], axis=1)


def weighted(found, top):
    spread = [found[:, p : p + 128] * FACTOR - top for p in range(0, found.shape[1], 128)]
    return jnp.concatenate([jnp.exp2(x).astype(BF16) for x in spread], axis=1)


def near_kernel(lengths_ref, queries_ref, own_ref, totals_ref, tops_ref, scores):
    tokens = queries_ref.shape[0]
    heads = queries_ref.shape[1] // DH
    base = lax.axis_index("ctx") * tokens
    bounds = bounds_of(lengths_ref)
    for block in range(tokens // ROWS):
        count = (block + 1) * ROWS
        rows = slice(block * ROWS, (block + 1) * ROWS)
        bias = bias_of(bounds, base + block * ROWS, ROWS, base, count)
        key, value = own_ref[:count, :], with_ones(own_ref[tokens : tokens + count, :])
        for h in range(heads):
            there = slice(h * ROWS, (h + 1) * ROWS)
            at = slice((block * heads + h) * ROWS, (block * heads + h + 1) * ROWS)
            found = lax.dot_general(
                queries_ref[rows, h * DH : (h + 1) * DH], key, NT, preferred_element_type=F32
            )
            found = found + bias
            scores[there, :count] = found
            top = found[:, :128]
            for p in range(128, count, 128):
                top = jnp.maximum(top, found[:, p : p + 128])
            top = jnp.max(top, axis=1, keepdims=True) * FACTOR + PLACED
            tops_ref[at, :] = jnp.broadcast_to(top, (ROWS, 128))
        for h in range(heads):
            there = slice(h * ROWS, (h + 1) * ROWS)
            at = slice((block * heads + h) * ROWS, (block * heads + h + 1) * ROWS)
            totals_ref[at, :] = jnp.dot(
                weighted(scores[there, :count], tops_ref[at, :]), value, preferred_element_type=F32
            )


def add_piece(bounds, base, block, origin, queries_ref, piece_ref, totals_ref, tops_ref):
    tokens = queries_ref.shape[0]
    heads = queries_ref.shape[1] // DH
    s = base + block * ROWS
    first = origin * tokens
    needed = (first < base) & (first + tokens > doc_start(bounds, s))
    whole = first >= doc_start(bounds, s + ROWS - 1)
    half = first + tokens <= doc_start(bounds, s + ROWS // 2)

    def add(bias, rows):
        key, value = piece_ref[:tokens, :], with_ones(piece_ref[tokens:, :])
        for h in range(heads):
            at = pl.ds(pl.multiple_of((block * heads + h) * ROWS, ROWS), rows)
            query = queries_ref[pl.ds(pl.multiple_of(block * ROWS, ROWS), rows), h * DH : (h + 1) * DH]
            found = lax.dot_general(query, key, NT, preferred_element_type=F32)
            if bias is not None:
                found = found + bias
            totals_ref[at, :] += jnp.dot(weighted(found, tops_ref[at, :]), value, preferred_element_type=F32)

    @pl.when(needed & whole)
    def _():
        add(None, ROWS)

    @pl.when(needed & jnp.logical_not(whole) & jnp.logical_not(half))
    def _():
        add(bias_of(bounds, s, ROWS, first, tokens), ROWS)

    @pl.when(needed & half)
    def _():
        add(bias_of(bounds, s, ROWS // 2, first, tokens), ROWS // 2)


def middle_kernel(count, which, lengths_ref, queries_ref, tops_ref, totals_in, *refs):
    pieces, totals_ref = refs[:-1], refs[-1]
    tokens = queries_ref.shape[0]
    base = lax.axis_index("ctx") * tokens
    bounds = bounds_of(lengths_ref)

    def row_block(block, _):
        for m, piece_ref in zip(which, pieces):
            add_piece(bounds, base, block, origin_of(m, count), queries_ref, piece_ref, totals_ref, tops_ref)
        return 0

    lax.fori_loop(0, tokens // ROWS, row_block, 0)


def last_kernel(count, which, lengths_ref, queries_ref, tops_ref, totals_in, *refs):
    pieces, out_ref, totals_ref = refs[:count], refs[count], refs[count + 1]
    tokens = queries_ref.shape[0]
    heads = queries_ref.shape[1] // DH
    base = lax.axis_index("ctx") * tokens
    bounds = bounds_of(lengths_ref)

    def row_block(block, _):
        for m in which:
            add_piece(bounds, base, block, origin_of(m, count), queries_ref, pieces[m], totals_ref, tops_ref)
        return 0

    lax.fori_loop(0, tokens // ROWS, row_block, 0)

    def divided(block, h):
        at = pl.ds(pl.multiple_of((block * heads + h) * ROWS, ROWS), ROWS)
        total = totals_ref[at, DH:]
        return (totals_ref[at, :DH] * pl.reciprocal(total, approx=True)).astype(BF16), total

    highest = jnp.zeros((ROWS, DH), F32)
    for block in range(tokens // ROWS):
        for h in range(heads):
            found, total = divided(block, h)
            out_ref[block * ROWS : (block + 1) * ROWS, h * DH : (h + 1) * DH] = found
            highest = jnp.maximum(highest, total)

    def again(block, h, at):
        s = base + block * ROWS
        rows = pl.ds(pl.multiple_of(block * ROWS, ROWS), ROWS)
        cols = pl.ds(pl.multiple_of(h * DH, DH), DH)
        query = queries_ref[rows, cols]

        def found_of(m):
            found = lax.dot_general(query, pieces[m][:tokens, :], NT, preferred_element_type=F32)
            return found + bias_of(bounds, s, ROWS, origin_of(m, count) * tokens, tokens)

        top = jnp.full((ROWS, 1), LOW, F32)
        for m in range(count):
            top = jnp.maximum(top, jnp.max(found_of(m), axis=1, keepdims=True))
        totals_ref[at, :] = jnp.zeros((ROWS, 2 * DH), F32)
        for m in range(count):
            weights = jnp.exp2((found_of(m) - top) * FACTOR).astype(BF16)
            totals_ref[at, :] += jnp.dot(weights, with_ones(pieces[m][tokens:, :]), preferred_element_type=F32)
        out_ref[rows, cols] = divided(block, h)[0]

    @pl.when(jnp.logical_not(jnp.max(highest) < 2.0**115))
    def _():
        def one(i, _):
            at = pl.ds(pl.multiple_of(i * ROWS, ROWS), ROWS)

            @pl.when(jnp.logical_not(jnp.max(totals_ref[at, DH:]) < 2.0**115))
            def _():
                again(i // heads, i % heads, at)

            return 0

        lax.fori_loop(0, tokens // ROWS * heads, one, 0)


def local(doc_lengths, lin_q, lin_k, lin_v, log_decay, lin_gain, soft_q, soft_k, soft_v):
    doc_lengths = doc_lengths.reshape(1, -1)
    tokens = lin_q.shape[0]
    heads = lin_gain.shape[0] // DH
    count = lax.axis_size("ctx")
    bits = count.bit_length() - 1
    blocks = tokens // BLK

    head_place = lax.axis_index("head")
    own_keys, own_values = soft_k, soft_v
    for bit in range((lax.axis_size("head") // KVH).bit_length() - 1):
        far_keys, far_values = swapped((own_keys, own_values), "head", bit)
        upper = head_place // (1 << bit) % 2 == 1

        def beside(own, far):
            return jnp.where(upper, jnp.concatenate([far, own], axis=1), jnp.concatenate([own, far], axis=1))

        own_keys, own_values = beside(own_keys, far_keys), beside(own_values, far_values)
    own = jnp.concatenate([own_keys, own_values], axis=0)
    own, lin_k = lax.optimization_barrier((own, lin_k))
    pieces = [own]
    for bit in range(bits):
        pieces = pieces + [swapped(piece, "ctx", bit) for piece in pieces]
        if bit == 0:
            pieces[1], queries_later = lax.optimization_barrier((pieces[1], lin_q))

    msg_rows = heads * DH + -(-2 * heads // 16) * 16
    msg = jax.ShapeDtypeStruct((msg_rows, DH), BF16)
    total, first, sums = pl.pallas_call(
        states_kernel,
        out_shape=(
            msg,
            jax.ShapeDtypeStruct((max(blocks - 1, 1), heads * DH, DH), BF16),
            jax.ShapeDtypeStruct(log_decay.shape, F32),
        ),
        in_specs=[VMEM, HBM, HBM, VMEM],
        out_specs=(VMEM,) * 3,
        scratch_shapes=[pltpu.VMEM(lin_k.shape, BF16)] * 2 + [pltpu.SemaphoreType.DMA((2, blocks))],
        cost_estimate=lasting(2.5),
        compiler_params=within(62),
        name="states",
    )(doc_lengths, lin_k, lin_v, log_decay)

    inside = pl.pallas_call(
        inside_kernel,
        out_shape=jax.ShapeDtypeStruct(lin_q.shape, BF16),
        in_specs=[VMEM] + [VMEM] * 4,
        out_specs=VMEM,
        cost_estimate=lasting(4),
        compiler_params=within(12),
        name="inside",
    )(doc_lengths, queries_later, lin_k, lin_v, sums)

    prefix = None
    for bit in range(bits - 1):
        far = swapped(total, "ctx", bit)
        if bit == 0:
            prefix = far
        else:
            prefix = pl.pallas_call(
                functools.partial(prefix_kernel, heads, bit),
                out_shape=msg,
                in_specs=[VMEM] * 2,
                out_specs=VMEM,
                compiler_params=within(8),
        name="prefix",
            )(prefix, far)
        total = pl.pallas_call(
            functools.partial(total_kernel, heads, bit),
            out_shape=msg,
            in_specs=[VMEM] * 2,
            out_specs=VMEM,
            cost_estimate=lasting(1),
            compiler_params=within(8),
        name="total",
        )(total, far)
    far = swapped(total, "ctx", bits - 1)

    totals = jax.ShapeDtypeStruct((heads * tokens, 2 * DH), F32)
    tops = jax.ShapeDtypeStruct((heads * tokens, 128), F32)
    totals, tops = pl.pallas_call(
        near_kernel,
        out_shape=(totals, tops),
        in_specs=[VMEM, VMEM, VMEM],
        out_specs=(VMEM, VMEM),
        scratch_shapes=[pltpu.VMEM((heads * ROWS, tokens), F32)],
        compiler_params=within(20),
        cost_estimate=lasting(4),
        name="near",
    )(doc_lengths, soft_q, pieces[0])
    early = [m for m in range(2, count) if m.bit_count() == 1]
    totals = pl.pallas_call(
        functools.partial(middle_kernel, count, early),
        out_shape=totals,
        in_specs=[VMEM] + [VMEM] * (3 + len(early)),
        out_specs=VMEM,
        input_output_aliases={3: 0},
        compiler_params=within(24),
        cost_estimate=lasting(4),
        name="middle",
    )(doc_lengths, soft_q, tops, totals, *[pieces[m] for m in early])
    late = [m for m in range(1, count) if m not in early]
    soft_out, _ = pl.pallas_call(
        functools.partial(last_kernel, count, late),
        out_shape=(jax.ShapeDtypeStruct(soft_q.shape, BF16), totals),
        in_specs=[VMEM] + [VMEM] * (3 + count),
        out_specs=(VMEM, VMEM),
        input_output_aliases={3: 1},
        compiler_params=within(24),
        cost_estimate=lasting(4),
        name="last",
    )(doc_lengths, soft_q, tops, totals, *pieces)

    wide = jax.ShapeDtypeStruct(lin_q.shape, BF16)
    return pl.pallas_call(
        functools.partial(across_kernel, bits - 1),
        out_shape=(wide, wide),
        in_specs=[VMEM] * 9,
        out_specs=(HBM, HBM),
        scratch_shapes=[pltpu.VMEM(lin_q.shape, BF16), pltpu.SemaphoreType.DMA((1 + blocks,))],
        compiler_params=within(12),
        cost_estimate=lasting(3),
        name="across",
    )(doc_lengths, lin_q, inside, sums, lin_gain.reshape(1, -1), first, prefix, far, soft_out)


def solution(mesh):
    rows = P("ctx", "head")
    placed = (P(), rows, rows, rows, P("head", "ctx"), P("head"), rows, rows, rows)
    return jax.shard_map(
        local, mesh=mesh, in_specs=placed, out_specs=(rows, rows), check_vma=False
    )
```

profile of v0, /device:TPU:0, one launch (start us, length us, event | category | flops | bytes accessed | tf_op | source)
XLA Modules:
  0.0 28.3 jit_solution(11772607880950848534)
XLA Ops:
  0.6 0.0 copy-start.6
  0.6 0.0 copy-start.2
  0.7 1.1 %pad_maximum_fusion.own_ref.refs_0_ = bf16[1024,128]{1,0:T(8,128)(2,1)S(1)} fusion(bf16[512,128]{1,0:T(8,128)(2,1)} %param.17, bf16[512,128]{1,0:T(8,128)(2,1)} %param.16), kind=kLoop, calls=%fused_computation | loop fusion | flops 524288 | bytes 524288 | tf_op jit(solution)/shard_map/concatenate | solution.py:445
  1.7 3.0 %collective-permute-start.3 = (bf16[1024,128]{1,0:T(8,128)(2,1)S(1)}, bf16[1024,128]{1,0:T(8,128)(2,1)S(1)}, u32[]{:S(2)}, u32[]{:S(2)}) collective-permute-start(bf16[1024,128]{1,0:T(8,128)(2,1)S(1)} %pad_maximum_fusion.own_ref.refs_0_), channel_id=1, source_target_pairs={{0,16},{8,24},{16,0},{24,8},{1,17},{9,25},{17,1},{25,9},{2,18},{10... | collective-permute-start | bytes 786440 | tf_op jit(solution)/shard_map/ppermute | solution.py:35
  4.8 1.5 %collective-permute-start = (bf16[1024,128]{1,0:T(8,128)(2,1)S(1)}, bf16[1024,128]{1,0:T(8,128)(2,1)S(1)}, u32[]{:S(2)}, u32[]{:S(2)}) collective-permute-start(bf16[1024,128]{1,0:T(8,128)(2,1)S(1)} %pad_maximum_fusion.own_ref.refs_0_), channel_id=1, source_target_pairs={{0,8},{8,0},{16,24},{24,16},{1,9},{9,1},{17,25},{25,17},{2,10},{10... | collective-permute-start | bytes 786440 | tf_op jit(solution)/shard_map/ppermute | solution.py:35
  6.3 3.4 %states.1 = (bf16[1040,128]{1,0:T(8,128)(2,1)}, bf16[1,1024,128]{2,1,0:T(8,128)(2,1)}, f32[8,512]{1,0:T(8,128)}) custom-call(s32[1,4]{1,0:T(1,128)} %bitcast.3, bf16[512,1024]{1,0:T(8,128)(2,1)} %keys_ref, bf16[512,1024]{1,0:T(8,128)(2,1)} %values_ref.1, f32[8,512]{1,0:T(8,128)} %decay_ref.1), custom_call_target="tpu_custom_call" | custom-call | flops 2000000000 | tf_op jit(solution)/shard_map/states/pallas_call | solution.py:455
  9.7 0.0 copy-start
  9.7 0.0 copy-start.1
  9.7 0.0 copy-start.3
  9.7 0.0 copy-start.8
  9.7 0.6 %collective-permute-start.1 = (bf16[1040,128]{1,0:T(8,128)(2,1)}, bf16[1040,128]{1,0:T(8,128)(2,1)S(1)}, u32[]{:S(2)}, u32[]{:S(2)}) collective-permute-start(bf16[1040,128]{1,0:T(8,128)(2,1)} %get-tuple-element.17.total_ref), channel_id=1, source_target_pairs={{0,8},{8,0},{16,24},{24,16},{1,9},{9,1},{17,25},{25,17},{2,10},{10... | collective-permute-start | bytes 798728 | tf_op jit(solution)/shard_map/ppermute | solution.py:35
  10.3 0.0 copy-done.6
  10.3 0.0 copy-done.2
  10.3 2.1 %near.1 = (f32[4096,256]{1,0:T(8,128)S(1)}, f32[4096,128]{1,0:T(8,128)S(1)}) custom-call(s32[1,4]{1,0:T(1,128)S(1)} %bitcast.4, bf16[512,1024]{1,0:T(8,128)(2,1)S(1)} %copy-done.2, bf16[1024,128]{1,0:T(8,128)(2,1)S(1)} %pad_maximum_fusion.own_ref.refs_0_), custom_call_target="tpu_custom_call" | custom-call | flops 3200000000 | tf_op jit(solution)/shard_map/near/pallas_call | solution.py:507
  12.5 0.7 %collective-permute-done.refs_1_ = bf16[1024,128]{1,0:T(8,128)(2,1)S(1)} collective-permute-done((bf16[1024,128]{1,0:T(8,128)(2,1)S(1)}, bf16[1024,128]{1,0:T(8,128)(2,1)S(1)}, u32[]{:S(2)}, u32[]{:S(2)}) %collective-permute-start) | collective-permute-done | bytes 262176 | tf_op jit(solution)/shard_map/ppermute | solution.py:35
  13.1 0.4 %collective-permute-start.4 = (bf16[1024,128]{1,0:T(8,128)(2,1)S(1)}, bf16[1024,128]{1,0:T(8,128)(2,1)S(1)}, u32[]{:S(2)}, u32[]{:S(2)}) collective-permute-start(bf16[1024,128]{1,0:T(8,128)(2,1)S(1)} %collective-permute-done.refs_1_), channel_id=1, source_target_pairs={{0,16},{8,24},{16,0},{24,8},{1,17},{9,25},{17,1},{25,9},{2,18},{10... | collective-permute-start | bytes 786440 | tf_op jit(solution)/shard_map/ppermute | solution.py:35
  13.5 0.0 copy-done
  13.5 0.0 copy-done.1
  13.5 0.0 copy-done.3
  13.5 0.0 copy-done.8
  13.5 1.8 %inside.1.inside_ref = bf16[512,1024]{1,0:T(8,128)(2,1)S(1)} custom-call(s32[1,4]{1,0:T(1,128)S(1)} %bitcast.5, bf16[512,1024]{1,0:T(8,128)(2,1)S(1)} %copy-done.3, bf16[512,1024]{1,0:T(8,128)(2,1)S(1)} %copy-done, bf16[512,1024]{1,0:T(8,128)(2,1)S(1)} %copy-done.1, f32[8,512]{1,0:T(8,128)S(1)} %copy-done.8), custom_call_target="tpu_custom_call" | custom-call | flops 3200000000 | tf_op jit(solution)/shard_map/inside/pallas_call | solution.py:470
  15.4 0.0 collective-permute-done.3.refs_0_.refs_2_
  15.4 0.0 copy-start.4
  15.4 0.4 %middle.1.totals_in = f32[4096,256]{1,0:T(8,128)S(1)} custom-call(s32[1,4]{1,0:T(1,128)S(1)} %bitcast.6, bf16[512,1024]{1,0:T(8,128)(2,1)S(1)} %copy-done.2, f32[4096,128]{1,0:T(8,128)S(1)} %get-tuple-element.18.tops_ref, f32[4096,256]{1,0:T(8,128)S(1)} %get-tuple-element.19.totals_in, ...), custom_call_target="tpu_custom_call", output_to_operand_aliasing={{}: (3, {})} | custom-call | flops 3200000000 | tf_op jit(solution)/shard_map/middle/pallas_call | solution.py:518
  15.8 2.5 %collective-permute-done.1.far_ref.prefix_ref = bf16[1040,128]{1,0:T(8,128)(2,1)S(1)} collective-permute-done((bf16[1040,128]{1,0:T(8,128)(2,1)}, bf16[1040,128]{1,0:T(8,128)(2,1)S(1)}, u32[]{:S(2)}, u32[]{:S(2)}) %collective-permute-start.1) | collective-permute-done | bytes 266272 | tf_op jit(solution)/shard_map/ppermute | solution.py:35
  18.2 0.0 copy-done.4
  18.2 0.2 total.1
  18.4 0.0 copy-start.5
  18.4 0.0 copy-start.7
  18.4 2.1 %collective-permute-start.2 = (bf16[1040,128]{1,0:T(8,128)(2,1)S(1)}, bf16[1040,128]{1,0:T(8,128)(2,1)S(1)}, u32[]{:S(2)}, u32[]{:S(2)}) collective-permute-start(bf16[1040,128]{1,0:T(8,128)(2,1)S(1)} %total.1), channel_id=1, source_target_pairs={{0,16},{8,24},{16,0},{24,8},{1,17},{9,25},{17,1},{25,9},{2,18},{10... | collective-permute-start | bytes 798728 | tf_op jit(solution)/shard_map/ppermute | solution.py:35
  20.5 0.0 collective-permute-done.4.refs_3_
  20.5 0.7 %last.1 = (bf16[512,1024]{1,0:T(8,128)(2,1)S(1)}, f32[4096,256]{1,0:T(8,128)S(1)}) custom-call(s32[1,4]{1,0:T(1,128)S(1)} %bitcast.7, bf16[512,1024]{1,0:T(8,128)(2,1)S(1)} %copy-done.2, f32[4096,128]{1,0:T(8,128)S(1)} %get-tuple-element.18.tops_ref, f32[4096,256]{1,0:T(8,128)S(1)} %middle.1.totals_in, ...), custom_call_target="tpu_custom_call", output_to_operand_aliasing={{1}: (3, {})} | custom-call | flops 3200000000 | tf_op jit(solution)/shard_map/last/pallas_call | solution.py:529
  21.2 4.6 %collective-permute-done.2.far_ref = bf16[1040,128]{1,0:T(8,128)(2,1)S(1)} collective-permute-done((bf16[1040,128]{1,0:T(8,128)(2,1)S(1)}, bf16[1040,128]{1,0:T(8,128)(2,1)S(1)}, u32[]{:S(2)}, u32[]{:S(2)}) %collective-permute-start.2) | collective-permute-done | bytes 266272 | tf_op jit(solution)/shard_map/ppermute | solution.py:35
  25.8 0.0 copy-done.5
  25.8 0.0 copy-done.7
  25.8 2.3 %across.1 = (bf16[512,1024]{1,0:T(8,128)(2,1)}, bf16[512,1024]{1,0:T(8,128)(2,1)}) custom-call(s32[1,4]{1,0:T(1,128)S(1)} %bitcast.8, bf16[512,1024]{1,0:T(8,128)(2,1)S(1)} %copy-done.3, bf16[512,1024]{1,0:T(8,128)(2,1)S(1)} %inside.1.inside_ref, f32[8,512]{1,0:T(8,128)S(1)} %copy-done.8, f32[1,1024]{1,0:T(1,128)S(1)} %bitcast.2, ...), custom_call_target="tpu_custom_call" | custom-call | flops 2400000000 | tf_op jit(solution)/shard_map/across/pallas_call | solution.py:541
Async XLA Ops:
  0.6 9.7 %copy-start.6 = (s32[4]{0:T(128)S(1)}, s32[4]{0:T(128)}, u32[]{:S(2)}) copy-start(s32[4]{0:T(128)} %param.9) | copy-start | bytes 52
  0.6 9.7 %copy-start.2 = (bf16[512,1024]{1,0:T(8,128)(2,1)S(1)}, bf16[512,1024]{1,0:T(8,128)(2,1)}, u32[]{:S(2)}) copy-start(bf16[512,1024]{1,0:T(8,128)(2,1)} %queries_ref.7) | copy-start | bytes 3145732
  1.7 13.6 %collective-permute-start.3 = (bf16[1024,128]{1,0:T(8,128)(2,1)S(1)}, bf16[1024,128]{1,0:T(8,128)(2,1)S(1)}, u32[]{:S(2)}, u32[]{:S(2)}) collective-permute-start(bf16[1024,128]{1,0:T(8,128)(2,1)S(1)} %pad_maximum_fusion.own_ref.refs_0_), channel_id=1, source_target_pairs={{0,16},{8,24},{16,0},{24,8},{1,17},{9,25},{17,1},{25,9},{2,18},{10... | collective-permute-start | bytes 786440 | tf_op jit(solution)/shard_map/ppermute | solution.py:35
  4.8 8.4 %collective-permute-start = (bf16[1024,128]{1,0:T(8,128)(2,1)S(1)}, bf16[1024,128]{1,0:T(8,128)(2,1)S(1)}, u32[]{:S(2)}, u32[]{:S(2)}) collective-permute-start(bf16[1024,128]{1,0:T(8,128)(2,1)S(1)} %pad_maximum_fusion.own_ref.refs_0_), channel_id=1, source_target_pairs={{0,8},{8,0},{16,24},{24,16},{1,9},{9,1},{17,25},{25,17},{2,10},{10... | collective-permute-start | bytes 786440 | tf_op jit(solution)/shard_map/ppermute | solution.py:35
  9.7 3.8 %copy-start = (bf16[512,1024]{1,0:T(8,128)(2,1)S(1)}, bf16[512,1024]{1,0:T(8,128)(2,1)}, u32[]{:S(2)}) copy-start(bf16[512,1024]{1,0:T(8,128)(2,1)} %keys_ref) | copy-start | bytes 3145732
  9.7 3.8 %copy-start.1 = (bf16[512,1024]{1,0:T(8,128)(2,1)S(1)}, bf16[512,1024]{1,0:T(8,128)(2,1)}, u32[]{:S(2)}) copy-start(bf16[512,1024]{1,0:T(8,128)(2,1)} %values_ref.1) | copy-start | bytes 3145732
  9.7 3.8 %copy-start.3 = (bf16[512,1024]{1,0:T(8,128)(2,1)S(1)}, bf16[512,1024]{1,0:T(8,128)(2,1)}, u32[]{:S(2)}) copy-start(bf16[512,1024]{1,0:T(8,128)(2,1)} %queries_ref.8) | copy-start | bytes 3145732
  9.7 3.8 %copy-start.8 = (f32[8,512]{1,0:T(8,128)S(1)}, f32[8,512]{1,0:T(8,128)}, u32[]{:S(2)}) copy-start(f32[8,512]{1,0:T(8,128)} %get-tuple-element.15.sums_ref) | copy-start | bytes 49156
  9.7 8.5 %collective-permute-start.1 = (bf16[1040,128]{1,0:T(8,128)(2,1)}, bf16[1040,128]{1,0:T(8,128)(2,1)S(1)}, u32[]{:S(2)}, u32[]{:S(2)}) collective-permute-start(bf16[1040,128]{1,0:T(8,128)(2,1)} %get-tuple-element.17.total_ref), channel_id=1, source_target_pairs={{0,8},{8,0},{16,24},{24,16},{1,9},{9,1},{17,25},{25,17},{2,10},{10... | collective-permute-start | bytes 798728 | tf_op jit(solution)/shard_map/ppermute | solution.py:35
  13.1 7.4 %collective-permute-start.4 = (bf16[1024,128]{1,0:T(8,128)(2,1)S(1)}, bf16[1024,128]{1,0:T(8,128)(2,1)S(1)}, u32[]{:S(2)}, u32[]{:S(2)}) collective-permute-start(bf16[1024,128]{1,0:T(8,128)(2,1)S(1)} %collective-permute-done.refs_1_), channel_id=1, source_target_pairs={{0,16},{8,24},{16,0},{24,8},{1,17},{9,25},{17,1},{25,9},{2,18},{10... | collective-permute-start | bytes 786440 | tf_op jit(solution)/shard_map/ppermute | solution.py:35
  15.4 2.9 %copy-start.4 = (bf16[1040,128]{1,0:T(8,128)(2,1)S(1)}, bf16[1040,128]{1,0:T(8,128)(2,1)}, u32[]{:S(2)}) copy-start(bf16[1040,128]{1,0:T(8,128)(2,1)} %get-tuple-element.17.total_ref) | copy-start | bytes 798724
  18.4 7.4 %copy-start.5 = (f32[1024]{0:T(1024)S(1)}, f32[1024]{0:T(1024)}, u32[]{:S(2)}) copy-start(f32[1024]{0:T(1024)} %param.14) | copy-start | bytes 12292
  18.4 7.4 %copy-start.7 = (bf16[1,1024,128]{2,1,0:T(8,128)(2,1)S(1)}, bf16[1,1024,128]{2,1,0:T(8,128)(2,1)}, u32[]{:S(2)}) copy-start(bf16[1,1024,128]{2,1,0:T(8,128)(2,1)} %get-tuple-element.16.first_ref) | copy-start | bytes 786436
  18.4 7.4 %collective-permute-start.2 = (bf16[1040,128]{1,0:T(8,128)(2,1)S(1)}, bf16[1040,128]{1,0:T(8,128)(2,1)S(1)}, u32[]{:S(2)}, u32[]{:S(2)}) collective-permute-start(bf16[1040,128]{1,0:T(8,128)(2,1)S(1)} %total.1), channel_id=1, source_target_pairs={{0,16},{8,24},{16,0},{24,8},{1,17},{9,25},{17,1},{25,9},{2,18},{10... | collective-permute-start | bytes 798728 | tf_op jit(solution)/shard_map/ppermute | solution.py:35
where the time goes:
time: 28.5 us; the launch traced here: 28.3 us
  Pallas kernels  10.9 us (38%)
  waiting for transfers between devices  7.7 us (27%)
  starting transfers between devices  7.6 us (27%)
  other arithmetic  1.08 us (4%)
  between operations  0.92 us (3%)
    ppermute x5, waiting for transfers between devices, swapped(): lax.ppermute(value, axis, [(i, i ^ 1 << bit) for i in range(lax.axis_size...  7.7 us
    ppermute x5, starting transfers between devices, swapped(): lax.ppermute(value, axis, [(i, i ^ 1 << bit) for i in range(lax.axis_size...  7.6 us
    pallas_call x1, Pallas kernels, local(): pl.pallas_call(states_kernel, out_shape=(msg, jax.ShapeDtypeStruct((max(b...  3.41 us
    pallas_call x1, Pallas kernels, local(): pl.pallas_call(functools.partial(across_kernel, bits - 1), out_shape=(wid...  2.29 us
    pallas_call x1, Pallas kernels, local(): pl.pallas_call(near_kernel, out_shape=(totals, tops), in_specs=[VMEM, VME...  2.13 us
    pallas_call x1, Pallas kernels, local(): pl.pallas_call(inside_kernel, out_shape=jax.ShapeDtypeStruct(lin_q.shape,...  1.83 us
    concatenate x1, other arithmetic, local(): own = jnp.concatenate([own_keys, own_values], axis=0)  1.08 us
    pallas_call x1, Pallas kernels, local(): pl.pallas_call(functools.partial(last_kernel, count, late), out_shape=(ja...  0.72 us
  transfers between devices with their start and end apart: 5, of which 3 were waited for; matrix products, arithmetic and copies ran while one was open for 0% of the time, Pallas kernels for 30%

commit v1 on v0

--- a/solution.py
+++ b/solution.py
@@ -27,6 +27,10 @@
     return pltpu.CompilerParams(vmem_limit_bytes=mib * 1024 * 1024)
 
 
+def in_hbm(array):
+    return pltpu.with_memory_space_constraint(array, pltpu.HBM)
+
+
 def lasting(us):
     return pl.CostEstimate(flops=int(us * 0.8e9), bytes_accessed=0, transcendentals=0)
 
@@ -80,6 +84,21 @@
     col = lax.broadcasted_iota(jnp.int32, (depth, heads * DH), 1)
     picks = jnp.where((row % heads == col // DH) & (row < count * heads), 1.0, 0.0).astype(BF16)
     return lax.dot_general(stacked.astype(BF16), picks, TN, preferred_element_type=F32)
+
+
+def fetch_kernel(keys, values, decay, lengths, own_ref, decay_ref, lengths_ref, sems):
+    tokens = keys.shape[0]
+    pairs = [
+        (keys, own_ref.at[pl.ds(0, tokens), :]),
+        (values, own_ref.at[pl.ds(tokens, tokens), :]),
+        (decay, decay_ref),
+        (lengths, lengths_ref),
+    ]
+    copies = [pltpu.make_async_copy(a, b, sems.at[i]) for i, (a, b) in enumerate(pairs)]
+    for copy in copies:
+        copy.start()
+    for copy in copies:
+        copy.wait()
 
 
 def states_kernel(lengths_ref, keys_hbm, values_hbm, decay_ref, msg_ref, first_ref, sums_ref, keys_ref, values_ref, sems):
@@ -130,7 +149,7 @@
     msg_ref[heads * DH :, :] = tail.astype(BF16)
 
 
-def inside_kernel(lengths_ref, queries_ref, keys_ref, values_ref, sums_ref, out_ref):
+def inside_kernel(lengths_ref, queries_ref, keys_ref, values_ref, sums_ref, out_ref, entering_ref):
     heads = sums_ref.shape[0]
     tokens = keys_ref.shape[0]
     base = lax.axis_index("ctx") * tokens
@@ -138,6 +157,7 @@
     rows = lax.broadcasted_iota(jnp.int32, (BLK, BLK), 0)
     cols = lax.broadcasted_iota(jnp.int32, (BLK, BLK), 1)
     place = lax.broadcasted_iota(jnp.int32, (BLK, 1), 0)
+    across = lax.broadcasted_iota(jnp.int32, (1, BLK), 1)
     for b in range(tokens // BLK):
         s = base + b * BLK
         start = doc_start(bounds, s + place) - s
@@ -145,6 +165,8 @@
         here = slice(b * BLK, (b + 1) * BLK)
         sums = sums_ref[:, here] * LOG2E
         down = over_lanes(sums, 3)
+        entering = jnp.where(doc_start(bounds, s + across) < s, jnp.exp2(sums), 0.0)
+        entering_ref[here, :] = over_lanes(entering, 2)
         for h in range(heads):
             there = slice(h * DH, (h + 1) * DH)
             upright = jnp.concatenate([down[:, there]] * (BLK // DH), axis=1)
@@ -217,7 +239,7 @@
 
 
 def across_kernel(
-    bit, lengths_ref, queries_ref, inside_ref, sums_ref, gain_ref, first_ref, prefix_ref, far_ref, soft_ref,
+    bit, lengths_ref, queries_ref, inside_ref, entering_ref, sums_ref, gain_ref, first_ref, prefix_ref, far_ref, soft_ref,
     out_hbm, soft_hbm, out_ref, sems,
 ):
     soft_copy = pltpu.make_async_copy(soft_ref, soft_hbm, sems.at[0])
@@ -230,31 +252,39 @@
     upper = jnp.where(upper_half(bit), 1.0, 0.0).astype(F32)
     valid = jnp.where(upper_half(0), 1.0, 0.0).astype(F32) if bit == 1 else 1.0
     bounds = bounds_of(lengths_ref)
-    place = lax.broadcasted_iota(jnp.int32, (1, BLK), 1)
     state = []
     for h in range(heads):
         here = slice(h * DH, (h + 1) * DH)
         through = upper * (valid * through_of(prefix_ref, heads, h) + (1.0 - valid))
         state.append(valid * prefix_ref[here, :].astype(F32) + through * far_ref[here, :].astype(F32))
-    ones = jnp.ones((DH, DH), BF16)
+    pair = 2 * DH
+    row = lax.broadcasted_iota(jnp.int32, (pair, pair), 0)
+    col = lax.broadcasted_iota(jnp.int32, (pair, pair), 1)
+    ones = jnp.where(row // DH == col // DH, 1.0, 0.0).astype(BF16)
+    zeros = jnp.zeros((DH, DH), BF16)
     for b in range(tokens // BLK):
         s = base + b * BLK
         here = slice(b * BLK, (b + 1) * BLK)
         start_last = doc_start(bounds, s + BLK - 1)
         kept = jnp.where(start_last < s, 1.0, 0.0).astype(F32)
-        sums = sums_ref[:, here]
-        factor = kept * jnp.exp(sums[:, BLK - 1 : BLK])
-        entering = jnp.where(doc_start(bounds, s + place) < s, jnp.exp(sums), 0.0)
-        entering = over_lanes(entering, 2)
-        for h in range(heads):
-            there = slice(h * DH, (h + 1) * DH)
-            across = jnp.dot(queries_ref[here, there], state[h].astype(BF16), preferred_element_type=F32)
-            raw = inside_ref[here, there].astype(F32) + across * entering[:, there]
+        factor = kept * jnp.exp(sums_ref[:, (b + 1) * BLK - 1 : (b + 1) * BLK])
+        for h in range(0, heads, 2):
+            there = slice(h * DH, (h + 2) * DH)
+            left = jnp.concatenate([state[h].astype(BF16), zeros], axis=1)
+            right = jnp.concatenate([zeros, state[h + 1].astype(BF16)], axis=1)
+            across = jnp.dot(
+                queries_ref[here, there],
+                jnp.concatenate([left, right], axis=0),
+                preferred_element_type=F32,
+            )
+            raw = inside_ref[here, there].astype(F32) + across * entering_ref[here, there]
             square = jnp.dot((raw * raw).astype(BF16), ones, preferred_element_type=F32)
             scale = lax.rsqrt(square * (1.0 / DH) + 1e-06)
             out_ref[here, there] = (raw * scale * gain_ref[:, there]).astype(BF16)
             if b < tokens // BLK - 1:
-                state[h] = factor[h : h + 1, :] * state[h] + first_ref[b, there, :].astype(F32)
+                for one in (h, h + 1):
+                    update = first_ref[b, one * DH : (one + 1) * DH, :].astype(F32)
+                    state[one] = factor[one : one + 1, :] * state[one] + update
         copies.append(pltpu.make_async_copy(out_ref.at[here, :], out_hbm.at[here, :], sems.at[1 + b]))
         copies[b].start()
     soft_copy.wait()
@@ -351,18 +381,14 @@
         add(bias_of(bounds, s, ROWS // 2, first, tokens), ROWS // 2)
 
 
-def middle_kernel(count, which, lengths_ref, queries_ref, tops_ref, totals_in, *refs):
+def middle_kernel(count, which, block, lengths_ref, queries_ref, tops_ref, totals_in, *refs):
     pieces, totals_ref = refs[:-1], refs[-1]
     tokens = queries_ref.shape[0]
     base = lax.axis_index("ctx") * tokens
     bounds = bounds_of(lengths_ref)
 
-    def row_block(block, _):
-        for m, piece_ref in zip(which, pieces):
-            add_piece(bounds, base, block, origin_of(m, count), queries_ref, piece_ref, totals_ref, tops_ref)
-        return 0
-
-    lax.fori_loop(0, tokens // ROWS, row_block, 0)
+    for m, piece in zip(which, pieces):
+        add_piece(bounds, base, block, origin_of(m, count), queries_ref, piece, totals_ref, tops_ref)
 
 
 def last_kernel(count, which, lengths_ref, queries_ref, tops_ref, totals_in, *refs):
@@ -442,7 +468,20 @@
             return jnp.where(upper, jnp.concatenate([far, own], axis=1), jnp.concatenate([own, far], axis=1))
 
         own_keys, own_values = beside(own_keys, far_keys), beside(own_values, far_values)
-    own = jnp.concatenate([own_keys, own_values], axis=0)
+    own, log_decay, doc_lengths = pl.pallas_call(
+        fetch_kernel,
+        out_shape=(
+            pltpu.VMEM((2 * tokens, DH), BF16),
+            pltpu.VMEM(log_decay.shape, F32),
+            pltpu.VMEM(doc_lengths.shape, jnp.int32),
+        ),
+        in_specs=[HBM] * 4,
+        out_specs=(VMEM,) * 3,
+        scratch_shapes=[pltpu.SemaphoreType.DMA((4,))],
+        compiler_params=within(2),
+        cost_estimate=lasting(1),
+        name="fetch",
+    )(in_hbm(own_keys), in_hbm(own_values), in_hbm(log_decay), in_hbm(doc_lengths))
     own, lin_k = lax.optimization_barrier((own, lin_k))
     pieces = [own]
     for bit in range(bits):
@@ -455,23 +494,37 @@
     total, first, sums = pl.pallas_call(
         states_kernel,
         out_shape=(
-            msg,
-            jax.ShapeDtypeStruct((max(blocks - 1, 1), heads * DH, DH), BF16),
-            jax.ShapeDtypeStruct(log_decay.shape, F32),
+            pltpu.VMEM(msg.shape, BF16),
+            pltpu.VMEM((max(blocks - 1, 1), heads * DH, DH), BF16),
+            pltpu.VMEM(log_decay.shape, F32),
         ),
         in_specs=[VMEM, HBM, HBM, VMEM],
         out_specs=(VMEM,) * 3,
         scratch_shapes=[pltpu.VMEM(lin_k.shape, BF16)] * 2 + [pltpu.SemaphoreType.DMA((2, blocks))],
         cost_estimate=lasting(2.5),
-        compiler_params=within(62),
+        compiler_params=within(12),
         name="states",
-    )(doc_lengths, lin_k, lin_v, log_decay)
-
-    inside = pl.pallas_call(
+    )(doc_lengths, in_hbm(lin_k), in_hbm(lin_v), log_decay)
+
+    totals = jax.ShapeDtypeStruct((heads * tokens, 2 * DH), F32)
+    tops = jax.ShapeDtypeStruct((heads * tokens, 128), F32)
+    totals, tops = pl.pallas_call(
+        near_kernel,
+        out_shape=(totals, tops),
+        in_specs=[VMEM, VMEM, VMEM],
+        out_specs=(VMEM, VMEM),
+        scratch_shapes=[pltpu.VMEM((heads * ROWS, tokens), F32)],
+        compiler_params=within(20),
+        cost_estimate=lasting(4),
+        name="near",
+    )(doc_lengths, soft_q, pieces[0])
+    total, tops = lax.optimization_barrier((total, tops))
+
+    inside, entering = pl.pallas_call(
         inside_kernel,
-        out_shape=jax.ShapeDtypeStruct(lin_q.shape, BF16),
+        out_shape=(pltpu.VMEM(lin_q.shape, BF16), pltpu.VMEM(lin_q.shape, F32)),
         in_specs=[VMEM] + [VMEM] * 4,
-        out_specs=VMEM,
+        out_specs=(VMEM, VMEM),
         cost_estimate=lasting(4),
         compiler_params=within(12),
         name="inside",
@@ -500,35 +553,31 @@
             compiler_params=within(8),
         name="total",
         )(total, far)
+
+    early = [m for m in range(2, count) if m.bit_count() == 1]
+    def middle(block, totals):
+        return pl.pallas_call(
+            functools.partial(middle_kernel, count, early, block),
+            out_shape=jax.ShapeDtypeStruct(totals.shape, F32),
+            in_specs=[VMEM] + [VMEM] * (3 + len(early)),
+            out_specs=VMEM,
+            input_output_aliases={3: 0},
+            compiler_params=within(24),
+            cost_estimate=lasting(2),
+            name="middle",
+        )(doc_lengths, soft_q, tops, totals, *[pieces[m] for m in early])
+
+    steps = tokens // ROWS
+    for block in range(steps // 2):
+        totals = middle(block, totals)
+    total, totals = lax.optimization_barrier((total, totals))
     far = swapped(total, "ctx", bits - 1)
-
-    totals = jax.ShapeDtypeStruct((heads * tokens, 2 * DH), F32)
-    tops = jax.ShapeDtypeStruct((heads * tokens, 128), F32)
-    totals, tops = pl.pallas_call(
-        near_kernel,
-        out_shape=(totals, tops),
-        in_specs=[VMEM, VMEM, VMEM],
-        out_specs=(VMEM, VMEM),
-        scratch_shapes=[pltpu.VMEM((heads * ROWS, tokens), F32)],
-        compiler_params=within(20),
-        cost_estimate=lasting(4),
-        name="near",
-    )(doc_lengths, soft_q, pieces[0])
-    early = [m for m in range(2, count) if m.bit_count() == 1]
-    totals = pl.pallas_call(
-        functools.partial(middle_kernel, count, early),
-        out_shape=totals,
-        in_specs=[VMEM] + [VMEM] * (3 + len(early)),
-        out_specs=VMEM,
-        input_output_aliases={3: 0},
-        compiler_params=within(24),
-        cost_estimate=lasting(4),
-        name="middle",
-    )(doc_lengths, soft_q, tops, totals, *[pieces[m] for m in early])
+    for block in range(steps // 2, steps):
+        totals = middle(block, totals)
     late = [m for m in range(1, count) if m not in early]
     soft_out, _ = pl.pallas_call(
         functools.partial(last_kernel, count, late),
-        out_shape=(jax.ShapeDtypeStruct(soft_q.shape, BF16), totals),
+        out_shape=(jax.ShapeDtypeStruct(soft_q.shape, BF16), jax.ShapeDtypeStruct(totals.shape, F32)),
         in_specs=[VMEM] + [VMEM] * (3 + count),
         out_specs=(VMEM, VMEM),
         input_output_aliases={3: 1},
@@ -541,13 +590,13 @@
     return pl.pallas_call(
         functools.partial(across_kernel, bits - 1),
         out_shape=(wide, wide),
-        in_specs=[VMEM] * 9,
+        in_specs=[VMEM] * 10,
         out_specs=(HBM, HBM),
         scratch_shapes=[pltpu.VMEM(lin_q.shape, BF16), pltpu.SemaphoreType.DMA((1 + blocks,))],
         compiler_params=within(12),
         cost_estimate=lasting(3),
         name="across",
-    )(doc_lengths, lin_q, inside, sums, lin_gain.reshape(1, -1), first, prefix, far, soft_out)
+    )(doc_lengths, lin_q, inside, entering, sums, lin_gain.reshape(1, -1), first, prefix, far, soft_out)
 
 
 def solution(mesh):

time: 28.5 us -> 27.9 us (0.979)
  waiting for transfers between devices: 7.7 us -> 9.65 us
  starting transfers between devices: 7.6 us -> 6.02 us
  other arithmetic: 1.08 us -> 0 us
    ppermute x5, waiting for transfers between devices: 7.7 us -> 9.65 us  [swapped(): lax.ppermute(value, axis, [(i, i ^ 1 << bit) for i in range(lax.axis_size...]
    ppermute x5, starting transfers between devices: 7.6 us -> 6.02 us  [swapped(): lax.ppermute(value, axis, [(i, i ^ 1 << bit) for i in range(lax.axis_size...]
    concatenate x1 -> x0, other arithmetic: 1.08 us -> none  [local(): own = jnp.concatenate([own_keys, own_values], axis=0)]
    pallas_call x3 -> x5, Pallas kernels: 5.62 us -> 6 us  [the longest x1 2.51 us: local(): pl.pallas_call(states_kernel, out_shape=(pltpu.VMEM(msg.shape, BF16), plt...]
    pallas_call x1, Pallas kernels: 2.29 us -> 1.97 us  [local(): pl.pallas_call(functools.partial(across_kernel, bits - 1), out_shape=(wid...]
  transfers between devices with their start and end apart: 5 -> 5, of which waited for: 3 -> 3; matrix products, arithmetic and copies ran while one was open for 0% -> 0% of each run, Pallas kernels for 30% -> 29%
where the time goes in v1:
time: 27.9 us; the launch traced here: 27.7 us
  Pallas kernels  11.1 us (40%)
  waiting for transfers between devices  9.65 us (35%)
  starting transfers between devices  6.02 us (22%)
  between operations  0.91 us (3%)
    ppermute x5, waiting for transfers between devices, swapped(): lax.ppermute(value, axis, [(i, i ^ 1 << bit) for i in range(lax.axis_size...  9.65 us
    ppermute x5, starting transfers between devices, swapped(): lax.ppermute(value, axis, [(i, i ^ 1 << bit) for i in range(lax.axis_size...  6.02 us
    pallas_call x1, Pallas kernels, local(): pl.pallas_call(states_kernel, out_shape=(pltpu.VMEM(msg.shape, BF16), plt...  2.51 us
    pallas_call x1, Pallas kernels, local(): pl.pallas_call(near_kernel, out_shape=(totals, tops), in_specs=[VMEM, VME...  2.25 us
    pallas_call x1, Pallas kernels, local(): pl.pallas_call(inside_kernel, out_shape=(pltpu.VMEM(lin_q.shape, BF16), p...  2.04 us
    pallas_call x1, Pallas kernels, local(): pl.pallas_call(functools.partial(across_kernel, bits - 1), out_shape=(wid...  1.97 us
    pallas_call x1, Pallas kernels, local(): pl.pallas_call(fetch_kernel, out_shape=(pltpu.VMEM((2 * tokens, DH), BF16...  1.01 us
    pallas_call x1, Pallas kernels, local(): pl.pallas_call(functools.partial(last_kernel, count, late), out_shape=(ja...  0.72 us
  transfers between devices with their start and end apart: 5, of which 3 were waited for; matrix products, arithmetic and copies ran while one was open for 0% of the time, Pallas kernels for 29%

profile of v1, /device:TPU:0, one launch (start us, length us, event | category | flops | bytes accessed | tf_op | source)
XLA Modules:
  0.0 27.7 jit_solution(2210776049624664716)
XLA Ops:
  0.6 1.0 %fetch.1 = (bf16[1024,128]{1,0:T(8,128)(2,1)S(1)}, f32[8,512]{1,0:T(8,128)S(1)}, s32[1,4]{1,0:T(1,128)S(1)}) custom-call(bf16[512,128]{1,0:T(8,128)(2,1)} %keys.1, bf16[512,128]{1,0:T(8,128)(2,1)} %values.1, f32[8,512]{1,0:T(8,128)} %decay.1, s32[1,4]{1,0:T(1,128)} %bitcast.3), custom_call_target="tpu_custom_call" | custom-call | flops 800000000 | tf_op jit(solution)/shard_map/fetch/pallas_call | solution.py:471
  1.6 0.0 copy-start
  1.7 3.0 %collective-permute-start.2 = (bf16[1024,128]{1,0:T(8,128)(2,1)S(1)}, bf16[1024,128]{1,0:T(8,128)(2,1)S(1)}, u32[]{:S(2)}, u32[]{:S(2)}) collective-permute-start(bf16[1024,128]{1,0:T(8,128)(2,1)S(1)} %get-tuple-element.23.own_ref.refs_0_), channel_id=1, source_target_pairs={{0,16},{8,24},{16,0},{24,8},{1,17},{9,25},{17,1},{25,9},{2,18},{10... | collective-permute-start | bytes 786440 | tf_op jit(solution)/shard_map/ppermute | solution.py:39
  4.7 1.5 %collective-permute-start = (bf16[1024,128]{1,0:T(8,128)(2,1)S(1)}, bf16[1024,128]{1,0:T(8,128)(2,1)S(1)}, u32[]{:S(2)}, u32[]{:S(2)}) collective-permute-start(bf16[1024,128]{1,0:T(8,128)(2,1)S(1)} %get-tuple-element.23.own_ref.refs_0_), channel_id=1, source_target_pairs={{0,8},{8,0},{16,24},{24,16},{1,9},{9,1},{17,25},{25,17},{2,10},{10... | collective-permute-start | bytes 786440 | tf_op jit(solution)/shard_map/ppermute | solution.py:39
  6.2 2.5 %states.1 = (bf16[1040,128]{1,0:T(8,128)(2,1)S(1)}, bf16[1,1024,128]{2,1,0:T(8,128)(2,1)S(1)}, f32[8,512]{1,0:T(8,128)S(1)}) custom-call(s32[1,4]{1,0:T(1,128)S(1)} %get-tuple-element.21.lengths_ref, bf16[512,1024]{1,0:T(8,128)(2,1)} %keys_ref, bf16[512,1024]{1,0:T(8,128)(2,1)} %values_ref.1, f32[8,512]{1,0:T(8,128)S(1)} %get-tuple-element.26.decay_ref), custom_call_target="tpu_custom_call" | custom-call | flops 2000000000 | tf_op jit(solution)/shard_map/states/pallas_call | solution.py:494
  8.7 0.0 copy-done
  8.7 0.0 copy-start.1
  8.7 0.0 copy-start.2
  8.7 0.0 copy-start.3
  8.7 2.2 %near.1 = (f32[4096,256]{1,0:T(8,128)S(1)}, f32[4096,128]{1,0:T(8,128)S(1)}) custom-call(s32[1,4]{1,0:T(1,128)S(1)} %get-tuple-element.21.lengths_ref, bf16[512,1024]{1,0:T(8,128)(2,1)S(1)} %copy-done, bf16[1024,128]{1,0:T(8,128)(2,1)S(1)} %get-tuple-element.23.own_ref.refs_0_), custom_call_target="tpu_custom_call" | custom-call | flops 3200000000 | tf_op jit(solution)/shard_map/near/pallas_call | solution.py:511
  11.0 0.6 %collective-permute-start.1 = (bf16[1040,128]{1,0:T(8,128)(2,1)S(1)}, bf16[1040,128]{1,0:T(8,128)(2,1)S(1)}, u32[]{:S(2)}, u32[]{:S(2)}) collective-permute-start(bf16[1040,128]{1,0:T(8,128)(2,1)S(1)} %get-tuple-element.33.total_ref), channel_id=1, source_target_pairs={{0,8},{8,0},{16,24},{24,16},{1,9},{9,1},{17,25},{25,17},{2,10},{10... | collective-permute-start | bytes 798728 | tf_op jit(solution)/shard_map/ppermute | solution.py:39
  11.6 0.8 %collective-permute-done.refs_1_ = bf16[1024,128]{1,0:T(8,128)(2,1)S(1)} collective-permute-done((bf16[1024,128]{1,0:T(8,128)(2,1)S(1)}, bf16[1024,128]{1,0:T(8,128)(2,1)S(1)}, u32[]{:S(2)}, u32[]{:S(2)}) %collective-permute-start) | collective-permute-done | bytes 262176 | tf_op jit(solution)/shard_map/ppermute | solution.py:39
  12.5 0.4 %collective-permute-start.4 = (bf16[1024,128]{1,0:T(8,128)(2,1)S(1)}, bf16[1024,128]{1,0:T(8,128)(2,1)S(1)}, u32[]{:S(2)}, u32[]{:S(2)}) collective-permute-start(bf16[1024,128]{1,0:T(8,128)(2,1)S(1)} %collective-permute-done.refs_1_), channel_id=1, source_target_pairs={{0,16},{8,24},{16,0},{24,8},{1,17},{9,25},{17,1},{25,9},{2,18},{10... | collective-permute-start | bytes 786440 | tf_op jit(solution)/shard_map/ppermute | solution.py:39
  12.8 0.0 copy-done.1
  12.8 0.0 copy-done.2
  12.8 0.0 copy-done.3
  12.8 2.0 %inside.1 = (bf16[512,1024]{1,0:T(8,128)(2,1)S(1)}, f32[512,1024]{1,0:T(8,128)S(1)}) custom-call(s32[1,4]{1,0:T(1,128)S(1)} %get-tuple-element.21.lengths_ref, bf16[512,1024]{1,0:T(8,128)(2,1)S(1)} %copy-done.3, bf16[512,1024]{1,0:T(8,128)(2,1)S(1)} %copy-done.1, bf16[512,1024]{1,0:T(8,128)(2,1)S(1)} %copy-done.2, f32[8,512]{1,0:T(8,128)S(1)} %get-tuple-element.27.sums_ref), custom_call_target="tpu_custom_call" | custom-call | flops 3200000000 | tf_op jit(solution)/shard_map/inside/pallas_call | solution.py:523
  14.9 0.0 collective-permute-done.2.refs_0_.refs_2_
  14.9 0.1 middle.2.totals_in
  15.0 3.7 %collective-permute-done.1.far_ref.prefix_ref = bf16[1040,128]{1,0:T(8,128)(2,1)S(1)} collective-permute-done((bf16[1040,128]{1,0:T(8,128)(2,1)S(1)}, bf16[1040,128]{1,0:T(8,128)(2,1)S(1)}, u32[]{:S(2)}, u32[]{:S(2)}) %collective-permute-start.1) | collective-permute-done | bytes 266272 | tf_op jit(solution)/shard_map/ppermute | solution.py:39
  18.7 0.2 total.1
  18.8 0.5 %collective-permute-start.3 = (bf16[1040,128]{1,0:T(8,128)(2,1)S(1)}, bf16[1040,128]{1,0:T(8,128)(2,1)S(1)}, u32[]{:S(2)}, u32[]{:S(2)}) collective-permute-start(bf16[1040,128]{1,0:T(8,128)(2,1)S(1)} %total.1), channel_id=1, source_target_pairs={{0,16},{8,24},{16,0},{24,8},{1,17},{9,25},{17,1},{25,9},{2,18},{10... | collective-permute-start | bytes 798728 | tf_op jit(solution)/shard_map/ppermute | solution.py:39
  19.4 0.3 %middle.3.totals_in = f32[4096,256]{1,0:T(8,128)S(1)} custom-call(s32[1,4]{1,0:T(1,128)S(1)} %get-tuple-element.21.lengths_ref, bf16[512,1024]{1,0:T(8,128)(2,1)S(1)} %copy-done, f32[4096,128]{1,0:T(8,128)S(1)} %get-tuple-element.34.tops_ref, f32[4096,256]{1,0:T(8,128)S(1)} %middle.2.totals_in, ...), custom_call_target="tpu_custom_call", output_to_operand_aliasing={{}: (3, {})} | custom-call | flops 1600000000 | tf_op jit(solution)/shard_map/middle/pallas_call | solution.py:559
  19.7 0.0 copy-start.4
  19.7 0.0 collective-permute-done.4.refs_3_
  19.7 0.7 %last.1 = (bf16[512,1024]{1,0:T(8,128)(2,1)S(1)}, f32[4096,256]{1,0:T(8,128)S(1)}) custom-call(s32[1,4]{1,0:T(1,128)S(1)} %get-tuple-element.21.lengths_ref, bf16[512,1024]{1,0:T(8,128)(2,1)S(1)} %copy-done, f32[4096,128]{1,0:T(8,128)S(1)} %get-tuple-element.34.tops_ref, f32[4096,256]{1,0:T(8,128)S(1)} %middle.3.totals_in, ...), custom_call_target="tpu_custom_call", output_to_operand_aliasing={{1}: (3, {})} | custom-call | flops 3200000000 | tf_op jit(solution)/shard_map/last/pallas_call | solution.py:578
  20.4 5.1 %collective-permute-done.3.far_ref = bf16[1040,128]{1,0:T(8,128)(2,1)S(1)} collective-permute-done((bf16[1040,128]{1,0:T(8,128)(2,1)S(1)}, bf16[1040,128]{1,0:T(8,128)(2,1)S(1)}, u32[]{:S(2)}, u32[]{:S(2)}) %collective-permute-start.3) | collective-permute-done | bytes 266272 | tf_op jit(solution)/shard_map/ppermute | solution.py:39
  25.6 0.0 copy-done.4
  25.6 2.0 %across.1 = (bf16[512,1024]{1,0:T(8,128)(2,1)}, bf16[512,1024]{1,0:T(8,128)(2,1)}) custom-call(s32[1,4]{1,0:T(1,128)S(1)} %get-tuple-element.21.lengths_ref, bf16[512,1024]{1,0:T(8,128)(2,1)S(1)} %copy-done.3, bf16[512,1024]{1,0:T(8,128)(2,1)S(1)} %get-tuple-element.28.inside_ref, f32[512,1024]{1,0:T(8,128)S(1)} %get-tuple-element.29.entering_ref, ...), custom_call_target="tpu_custom_call" | custom-call | flops 2400000000 | tf_op jit(solution)/shard_map/across/pallas_call | solution.py:590
Async XLA Ops:
  1.6 7.1 %copy-start = (bf16[512,1024]{1,0:T(8,128)(2,1)S(1)}, bf16[512,1024]{1,0:T(8,128)(2,1)}, u32[]{:S(2)}) copy-start(bf16[512,1024]{1,0:T(8,128)(2,1)} %queries_ref.9) | copy-start | bytes 3145732
  1.7 13.2 %collective-permute-start.2 = (bf16[1024,128]{1,0:T(8,128)(2,1)S(1)}, bf16[1024,128]{1,0:T(8,128)(2,1)S(1)}, u32[]{:S(2)}, u32[]{:S(2)}) collective-permute-start(bf16[1024,128]{1,0:T(8,128)(2,1)S(1)} %get-tuple-element.23.own_ref.refs_0_), channel_id=1, source_target_pairs={{0,16},{8,24},{16,0},{24,8},{1,17},{9,25},{17,1},{25,9},{2,18},{10... | collective-permute-start | bytes 786440 | tf_op jit(solution)/shard_map/ppermute | solution.py:39
  4.7 7.8 %collective-permute-start = (bf16[1024,128]{1,0:T(8,128)(2,1)S(1)}, bf16[1024,128]{1,0:T(8,128)(2,1)S(1)}, u32[]{:S(2)}, u32[]{:S(2)}) collective-permute-start(bf16[1024,128]{1,0:T(8,128)(2,1)S(1)} %get-tuple-element.23.own_ref.refs_0_), channel_id=1, source_target_pairs={{0,8},{8,0},{16,24},{24,16},{1,9},{9,1},{17,25},{25,17},{2,10},{10... | collective-permute-start | bytes 786440 | tf_op jit(solution)/shard_map/ppermute | solution.py:39
  8.7 4.1 %copy-start.1 = (bf16[512,1024]{1,0:T(8,128)(2,1)S(1)}, bf16[512,1024]{1,0:T(8,128)(2,1)}, u32[]{:S(2)}) copy-start(bf16[512,1024]{1,0:T(8,128)(2,1)} %keys_ref) | copy-start | bytes 3145732
  8.7 4.1 %copy-start.2 = (bf16[512,1024]{1,0:T(8,128)(2,1)S(1)}, bf16[512,1024]{1,0:T(8,128)(2,1)}, u32[]{:S(2)}) copy-start(bf16[512,1024]{1,0:T(8,128)(2,1)} %values_ref.1) | copy-start | bytes 3145732
  8.7 4.1 %copy-start.3 = (bf16[512,1024]{1,0:T(8,128)(2,1)S(1)}, bf16[512,1024]{1,0:T(8,128)(2,1)}, u32[]{:S(2)}) copy-start(bf16[512,1024]{1,0:T(8,128)(2,1)} %queries_ref.10) | copy-start | bytes 3145732
  11.0 7.7 %collective-permute-start.1 = (bf16[1040,128]{1,0:T(8,128)(2,1)S(1)}, bf16[1040,128]{1,0:T(8,128)(2,1)S(1)}, u32[]{:S(2)}, u32[]{:S(2)}) collective-permute-start(bf16[1040,128]{1,0:T(8,128)(2,1)S(1)} %get-tuple-element.33.total_ref), channel_id=1, source_target_pairs={{0,8},{8,0},{16,24},{24,16},{1,9},{9,1},{17,25},{25,17},{2,10},{10... | collective-permute-start | bytes 798728 | tf_op jit(solution)/shard_map/ppermute | solution.py:39
  12.5 7.3 %collective-permute-start.4 = (bf16[1024,128]{1,0:T(8,128)(2,1)S(1)}, bf16[1024,128]{1,0:T(8,128)(2,1)S(1)}, u32[]{:S(2)}, u32[]{:S(2)}) collective-permute-start(bf16[1024,128]{1,0:T(8,128)(2,1)S(1)} %collective-permute-done.refs_1_), channel_id=1, source_target_pairs={{0,16},{8,24},{16,0},{24,8},{1,17},{9,25},{17,1},{25,9},{2,18},{10... | collective-permute-start | bytes 786440 | tf_op jit(solution)/shard_map/ppermute | solution.py:39
  18.8 6.7 %collective-permute-start.3 = (bf16[1040,128]{1,0:T(8,128)(2,1)S(1)}, bf16[1040,128]{1,0:T(8,128)(2,1)S(1)}, u32[]{:S(2)}, u32[]{:S(2)}) collective-permute-start(bf16[1040,128]{1,0:T(8,128)(2,1)S(1)} %total.1), channel_id=1, source_target_pairs={{0,16},{8,24},{16,0},{24,8},{1,17},{9,25},{17,1},{25,9},{2,18},{10... | collective-permute-start | bytes 798728 | tf_op jit(solution)/shard_map/ppermute | solution.py:39
  19.7 5.9 %copy-start.4 = (f32[1024]{0:T(1024)S(1)}, f32[1024]{0:T(1024)}, u32[]{:S(2)}) copy-start(f32[1024]{0:T(1024)} %param.14) | copy-start | bytes 12292

commit v2 on v1

--- a/solution.py
+++ b/solution.py
@@ -488,6 +488,7 @@
         pieces = pieces + [swapped(piece, "ctx", bit) for piece in pieces]
         if bit == 0:
             pieces[1], queries_later = lax.optimization_barrier((pieces[1], lin_q))
+            pieces[0], doc_lengths = lax.optimization_barrier((pieces[0], jnp.maximum(doc_lengths, 1)))
 
     msg_rows = heads * DH + -(-2 * heads // 16) * 16
     msg = jax.ShapeDtypeStruct((msg_rows, DH), BF16)
@@ -505,20 +506,6 @@
         compiler_params=within(12),
         name="states",
     )(doc_lengths, in_hbm(lin_k), in_hbm(lin_v), log_decay)
-
-    totals = jax.ShapeDtypeStruct((heads * tokens, 2 * DH), F32)
-    tops = jax.ShapeDtypeStruct((heads * tokens, 128), F32)
-    totals, tops = pl.pallas_call(
-        near_kernel,
-        out_shape=(totals, tops),
-        in_specs=[VMEM, VMEM, VMEM],
-        out_specs=(VMEM, VMEM),
-        scratch_shapes=[pltpu.VMEM((heads * ROWS, tokens), F32)],
-        compiler_params=within(20),
-        cost_estimate=lasting(4),
-        name="near",
-    )(doc_lengths, soft_q, pieces[0])
-    total, tops = lax.optimization_barrier((total, tops))
 
     inside, entering = pl.pallas_call(
         inside_kernel,
@@ -554,6 +541,18 @@
         name="total",
         )(total, far)
 
+    totals = jax.ShapeDtypeStruct((heads * tokens, 2 * DH), F32)
+    tops = jax.ShapeDtypeStruct((heads * tokens, 128), F32)
+    totals, tops = pl.pallas_call(
+        near_kernel,
+        out_shape=(totals, tops),
+        in_specs=[VMEM, VMEM, VMEM],
+        out_specs=(VMEM, VMEM),
+        scratch_shapes=[pltpu.VMEM((heads * ROWS, tokens), F32)],
+        compiler_params=within(20),
+        cost_estimate=lasting(4),
+        name="near",
+    )(doc_lengths, soft_q, pieces[0])
     early = [m for m in range(2, count) if m.bit_count() == 1]
     def middle(block, totals):
         return pl.pallas_call(

time: 27.9 us -> 26.9 us (0.964)
  waiting for transfers between devices: 9.65 us -> 5.46 us
  starting transfers between devices: 6.02 us -> 9.22 us
    ppermute x5, waiting for transfers between devices: 9.65 us -> 5.46 us  [swapped(): lax.ppermute(value, axis, [(i, i ^ 1 << bit) for i in range(lax.axis_size...]
    ppermute x5, starting transfers between devices: 6.02 us -> 9.22 us  [swapped(): lax.ppermute(value, axis, [(i, i ^ 1 << bit) for i in range(lax.axis_size...]
  transfers between devices with their start and end apart: 5 -> 5, of which waited for: 3 -> 3; matrix products, arithmetic and copies ran while one was open for 0% -> 0% of each run, Pallas kernels for 29% -> 30%
where the time goes in v2:
time: 26.9 us; the launch traced here: 26.7 us
  Pallas kernels  11.1 us (41%)
  starting transfers between devices  9.22 us (34%)
  waiting for transfers between devices  5.46 us (20%)
  between operations  0.91 us (3%)
    ppermute x5, starting transfers between devices, swapped(): lax.ppermute(value, axis, [(i, i ^ 1 << bit) for i in range(lax.axis_size...  9.22 us
    ppermute x5, waiting for transfers between devices, swapped(): lax.ppermute(value, axis, [(i, i ^ 1 << bit) for i in range(lax.axis_size...  5.46 us
    pallas_call x1, Pallas kernels, local(): pl.pallas_call(states_kernel, out_shape=(pltpu.VMEM(msg.shape, BF16), plt...  2.52 us
    pallas_call x1, Pallas kernels, local(): pl.pallas_call(near_kernel, out_shape=(totals, tops), in_specs=[VMEM, VME...  2.25 us
    pallas_call x1, Pallas kernels, local(): pl.pallas_call(inside_kernel, out_shape=(pltpu.VMEM(lin_q.shape, BF16), p...  2.04 us
    pallas_call x1, Pallas kernels, local(): pl.pallas_call(functools.partial(across_kernel, bits - 1), out_shape=(wid...  1.97 us
    pallas_call x1, Pallas kernels, local(): pl.pallas_call(fetch_kernel, out_shape=(pltpu.VMEM((2 * tokens, DH), BF16...  1.01 us
    pallas_call x1, Pallas kernels, local(): pl.pallas_call(functools.partial(last_kernel, count, late), out_shape=(ja...  0.71 us
  transfers between devices with their start and end apart: 5, of which 3 were waited for; matrix products, arithmetic and copies ran while one was open for 0% of the time, Pallas kernels for 30%

profile of v2, /device:TPU:0, one launch (start us, length us, event | category | flops | bytes accessed | tf_op | source)
XLA Modules:
  0.0 26.7 jit_solution(13074284904497961131)
XLA Ops:
  0.6 1.0 %fetch.1 = (bf16[1024,128]{1,0:T(8,128)(2,1)S(1)}, f32[8,512]{1,0:T(8,128)S(1)}, s32[1,4]{1,0:T(1,128)S(1)}) custom-call(bf16[512,128]{1,0:T(8,128)(2,1)} %keys.1, bf16[512,128]{1,0:T(8,128)(2,1)} %values.1, f32[8,512]{1,0:T(8,128)} %decay.1, s32[1,4]{1,0:T(1,128)} %bitcast.3), custom_call_target="tpu_custom_call" | custom-call | flops 800000000 | tf_op jit(solution)/shard_map/fetch/pallas_call | solution.py:471
  1.6 0.0 copy-start
  1.7 3.0 %collective-permute-start = (bf16[1024,128]{1,0:T(8,128)(2,1)S(1)}, bf16[1024,128]{1,0:T(8,128)(2,1)S(1)}, u32[]{:S(2)}, u32[]{:S(2)}) collective-permute-start(bf16[1024,128]{1,0:T(8,128)(2,1)S(1)} %get-tuple-element.33.own_ref.refs_0_), channel_id=1, source_target_pairs={{0,8},{8,0},{16,24},{24,16},{1,9},{9,1},{17,25},{25,17},{2,10},{10... | collective-permute-start | bytes 786440 | tf_op jit(solution)/shard_map/ppermute | solution.py:39
  4.7 1.5 %collective-permute-start.2 = (bf16[1024,128]{1,0:T(8,128)(2,1)S(1)}, bf16[1024,128]{1,0:T(8,128)(2,1)S(1)}, u32[]{:S(2)}, u32[]{:S(2)}) collective-permute-start(bf16[1024,128]{1,0:T(8,128)(2,1)S(1)} %get-tuple-element.33.own_ref.refs_0_), channel_id=1, source_target_pairs={{0,16},{8,24},{16,0},{24,8},{1,17},{9,25},{17,1},{25,9},{2,18},{10... | collective-permute-start | bytes 786440 | tf_op jit(solution)/shard_map/ppermute | solution.py:39
  6.2 2.5 %states.1 = (bf16[1040,128]{1,0:T(8,128)(2,1)S(1)}, bf16[1,1024,128]{2,1,0:T(8,128)(2,1)S(1)}, f32[8,512]{1,0:T(8,128)S(1)}) custom-call(s32[1,4]{1,0:T(1,128)S(1)} %broadcast_maximum_fusion.lengths_ref, bf16[512,1024]{1,0:T(8,128)(2,1)} %keys_ref, bf16[512,1024]{1,0:T(8,128)(2,1)} %values_ref.1, f32[8,512]{1,0:T(8,128)S(1)} %get-tuple-element.27.decay_ref), custom_call_target="tpu_custom_call" | custom-call | flops 2000000000 | tf_op jit(solution)/shard_map/states/pallas_call | solution.py:495
  8.7 0.0 copy-start.1
  8.7 0.0 copy-start.2
  8.7 0.0 copy-start.3
  8.7 0.6 %collective-permute-start.1 = (bf16[1040,128]{1,0:T(8,128)(2,1)S(1)}, bf16[1040,128]{1,0:T(8,128)(2,1)S(1)}, u32[]{:S(2)}, u32[]{:S(2)}) collective-permute-start(bf16[1040,128]{1,0:T(8,128)(2,1)S(1)} %get-tuple-element.32.total_ref), channel_id=1, source_target_pairs={{0,8},{8,0},{16,24},{24,16},{1,9},{9,1},{17,25},{25,17},{2,10},{10... | collective-permute-start | bytes 798728 | tf_op jit(solution)/shard_map/ppermute | solution.py:39
  9.3 0.0 copy-done
  9.3 2.2 %near.1 = (f32[4096,256]{1,0:T(8,128)S(1)}, f32[4096,128]{1,0:T(8,128)S(1)}) custom-call(s32[1,4]{1,0:T(1,128)S(1)} %broadcast_maximum_fusion.lengths_ref, bf16[512,1024]{1,0:T(8,128)(2,1)S(1)} %copy-done, bf16[1024,128]{1,0:T(8,128)(2,1)S(1)} %get-tuple-element.33.own_ref.refs_0_), custom_call_target="tpu_custom_call" | custom-call | flops 3200000000 | tf_op jit(solution)/shard_map/near/pallas_call | solution.py:546
  11.6 0.0 collective-permute-done.refs_1_
  11.6 2.3 %collective-permute-start.4 = (bf16[1024,128]{1,0:T(8,128)(2,1)S(1)}, bf16[1024,128]{1,0:T(8,128)(2,1)S(1)}, u32[]{:S(2)}, u32[]{:S(2)}) collective-permute-start(bf16[1024,128]{1,0:T(8,128)(2,1)S(1)} %collective-permute-done.refs_1_), channel_id=1, source_target_pairs={{0,16},{8,24},{16,0},{24,8},{1,17},{9,25},{17,1},{25,9},{2,18},{10... | collective-permute-start | bytes 786440 | tf_op jit(solution)/shard_map/ppermute | solution.py:39
  13.9 0.0 copy-done.1
  13.9 0.0 copy-done.2
  13.9 0.0 copy-done.3
  13.9 2.0 %inside.1 = (bf16[512,1024]{1,0:T(8,128)(2,1)S(1)}, f32[512,1024]{1,0:T(8,128)S(1)}) custom-call(s32[1,4]{1,0:T(1,128)S(1)} %broadcast_maximum_fusion.lengths_ref, bf16[512,1024]{1,0:T(8,128)(2,1)S(1)} %copy-done.3, bf16[512,1024]{1,0:T(8,128)(2,1)S(1)} %copy-done.1, bf16[512,1024]{1,0:T(8,128)(2,1)S(1)} %copy-done.2, f32[8,512]{1,0:T(8,128)S(1)} %get-tuple-element.28.sums_ref), custom_call_target="tpu_custom_call" | custom-call | flops 3200000000 | tf_op jit(solution)/shard_map/inside/pallas_call | solution.py:510
  15.9 0.0 collective-permute-done.2.refs_0_.refs_2_
  15.9 0.1 middle.2.totals_in
  16.1 0.6 %collective-permute-done.1.far_ref.prefix_ref = bf16[1040,128]{1,0:T(8,128)(2,1)S(1)} collective-permute-done((bf16[1040,128]{1,0:T(8,128)(2,1)S(1)}, bf16[1040,128]{1,0:T(8,128)(2,1)S(1)}, u32[]{:S(2)}, u32[]{:S(2)}) %collective-permute-start.1) | collective-permute-done | bytes 266272 | tf_op jit(solution)/shard_map/ppermute | solution.py:39
  16.7 0.2 total.1
  16.8 1.8 %collective-permute-start.3 = (bf16[1040,128]{1,0:T(8,128)(2,1)S(1)}, bf16[1040,128]{1,0:T(8,128)(2,1)S(1)}, u32[]{:S(2)}, u32[]{:S(2)}) collective-permute-start(bf16[1040,128]{1,0:T(8,128)(2,1)S(1)} %total.1), channel_id=1, source_target_pairs={{0,16},{8,24},{16,0},{24,8},{1,17},{9,25},{17,1},{25,9},{2,18},{10... | collective-permute-start | bytes 798728 | tf_op jit(solution)/shard_map/ppermute | solution.py:39
  18.7 0.3 %middle.3.totals_in = f32[4096,256]{1,0:T(8,128)S(1)} custom-call(s32[1,4]{1,0:T(1,128)S(1)} %broadcast_maximum_fusion.lengths_ref, bf16[512,1024]{1,0:T(8,128)(2,1)S(1)} %copy-done, f32[4096,128]{1,0:T(8,128)S(1)} %get-tuple-element.34.tops_ref, f32[4096,256]{1,0:T(8,128)S(1)} %middle.2.totals_in, ...), custom_call_target="tpu_custom_call", output_to_operand_aliasing={{}: (3, {})} | custom-call | flops 1600000000 | tf_op jit(solution)/shard_map/middle/pallas_call | solution.py:558
  19.0 0.0 copy-start.4
  19.0 0.2 collective-permute-done.4.refs_3_
  19.2 0.7 %last.1 = (bf16[512,1024]{1,0:T(8,128)(2,1)S(1)}, f32[4096,256]{1,0:T(8,128)S(1)}) custom-call(s32[1,4]{1,0:T(1,128)S(1)} %broadcast_maximum_fusion.lengths_ref, bf16[512,1024]{1,0:T(8,128)(2,1)S(1)} %copy-done, f32[4096,128]{1,0:T(8,128)S(1)} %get-tuple-element.34.tops_ref, f32[4096,256]{1,0:T(8,128)S(1)} %middle.3.totals_in, ...), custom_call_target="tpu_custom_call", output_to_operand_aliasing={{1}: (3, {})} | custom-call | flops 3200000000 | tf_op jit(solution)/shard_map/last/pallas_call | solution.py:577
  19.9 4.7 %collective-permute-done.3.far_ref = bf16[1040,128]{1,0:T(8,128)(2,1)S(1)} collective-permute-done((bf16[1040,128]{1,0:T(8,128)(2,1)S(1)}, bf16[1040,128]{1,0:T(8,128)(2,1)S(1)}, u32[]{:S(2)}, u32[]{:S(2)}) %collective-permute-start.3) | collective-permute-done | bytes 266272 | tf_op jit(solution)/shard_map/ppermute | solution.py:39
  24.6 0.0 copy-done.4
  24.6 2.0 %across.1 = (bf16[512,1024]{1,0:T(8,128)(2,1)}, bf16[512,1024]{1,0:T(8,128)(2,1)}) custom-call(s32[1,4]{1,0:T(1,128)S(1)} %broadcast_maximum_fusion.lengths_ref, bf16[512,1024]{1,0:T(8,128)(2,1)S(1)} %copy-done.3, bf16[512,1024]{1,0:T(8,128)(2,1)S(1)} %get-tuple-element.29.inside_ref, f32[512,1024]{1,0:T(8,128)S(1)} %get-tuple-element.30.entering_ref, ...), custom_call_target="tpu_custom_call" | custom-call | flops 2400000000 | tf_op jit(solution)/shard_map/across/pallas_call | solution.py:589
  (1 shorter events, 0.0 us)
Async XLA Ops:
  1.6 7.7 %copy-start = (bf16[512,1024]{1,0:T(8,128)(2,1)S(1)}, bf16[512,1024]{1,0:T(8,128)(2,1)}, u32[]{:S(2)}) copy-start(bf16[512,1024]{1,0:T(8,128)(2,1)} %queries_ref.9) | copy-start | bytes 3145732
  1.7 9.9 %collective-permute-start = (bf16[1024,128]{1,0:T(8,128)(2,1)S(1)}, bf16[1024,128]{1,0:T(8,128)(2,1)S(1)}, u32[]{:S(2)}, u32[]{:S(2)}) collective-permute-start(bf16[1024,128]{1,0:T(8,128)(2,1)S(1)} %get-tuple-element.33.own_ref.refs_0_), channel_id=1, source_target_pairs={{0,8},{8,0},{16,24},{24,16},{1,9},{9,1},{17,25},{25,17},{2,10},{10... | collective-permute-start | bytes 786440 | tf_op jit(solution)/shard_map/ppermute | solution.py:39
  4.7 11.3 %collective-permute-start.2 = (bf16[1024,128]{1,0:T(8,128)(2,1)S(1)}, bf16[1024,128]{1,0:T(8,128)(2,1)S(1)}, u32[]{:S(2)}, u32[]{:S(2)}) collective-permute-start(bf16[1024,128]{1,0:T(8,128)(2,1)S(1)} %get-tuple-element.33.own_ref.refs_0_), channel_id=1, source_target_pairs={{0,16},{8,24},{16,0},{24,8},{1,17},{9,25},{17,1},{25,9},{2,18},{10... | collective-permute-start | bytes 786440 | tf_op jit(solution)/shard_map/ppermute | solution.py:39
  8.7 5.2 %copy-start.1 = (bf16[512,1024]{1,0:T(8,128)(2,1)S(1)}, bf16[512,1024]{1,0:T(8,128)(2,1)}, u32[]{:S(2)}) copy-start(bf16[512,1024]{1,0:T(8,128)(2,1)} %keys_ref) | copy-start | bytes 3145732
  8.7 5.2 %copy-start.2 = (bf16[512,1024]{1,0:T(8,128)(2,1)S(1)}, bf16[512,1024]{1,0:T(8,128)(2,1)}, u32[]{:S(2)}) copy-start(bf16[512,1024]{1,0:T(8,128)(2,1)} %values_ref.1) | copy-start | bytes 3145732
  8.7 5.2 %copy-start.3 = (bf16[512,1024]{1,0:T(8,128)(2,1)S(1)}, bf16[512,1024]{1,0:T(8,128)(2,1)}, u32[]{:S(2)}) copy-start(bf16[512,1024]{1,0:T(8,128)(2,1)} %queries_ref.10) | copy-start | bytes 3145732
  8.7 7.9 %collective-permute-start.1 = (bf16[1040,128]{1,0:T(8,128)(2,1)S(1)}, bf16[1040,128]{1,0:T(8,128)(2,1)S(1)}, u32[]{:S(2)}, u32[]{:S(2)}) collective-permute-start(bf16[1040,128]{1,0:T(8,128)(2,1)S(1)} %get-tuple-element.32.total_ref), channel_id=1, source_target_pairs={{0,8},{8,0},{16,24},{24,16},{1,9},{9,1},{17,25},{25,17},{2,10},{10... | collective-permute-start | bytes 798728 | tf_op jit(solution)/shard_map/ppermute | solution.py:39
  11.6 7.6 %collective-permute-start.4 = (bf16[1024,128]{1,0:T(8,128)(2,1)S(1)}, bf16[1024,128]{1,0:T(8,128)(2,1)S(1)}, u32[]{:S(2)}, u32[]{:S(2)}) collective-permute-start(bf16[1024,128]{1,0:T(8,128)(2,1)S(1)} %collective-permute-done.refs_1_), channel_id=1, source_target_pairs={{0,16},{8,24},{16,0},{24,8},{1,17},{9,25},{17,1},{25,9},{2,18},{10... | collective-permute-start | bytes 786440 | tf_op jit(solution)/shard_map/ppermute | solution.py:39
  16.8 7.8 %collective-permute-start.3 = (bf16[1040,128]{1,0:T(8,128)(2,1)S(1)}, bf16[1040,128]{1,0:T(8,128)(2,1)S(1)}, u32[]{:S(2)}, u32[]{:S(2)}) collective-permute-start(bf16[1040,128]{1,0:T(8,128)(2,1)S(1)} %total.1), channel_id=1, source_target_pairs={{0,16},{8,24},{16,0},{24,8},{1,17},{9,25},{17,1},{25,9},{2,18},{10... | collective-permute-start | bytes 798728 | tf_op jit(solution)/shard_map/ppermute | solution.py:39
  19.0 5.6 %copy-start.4 = (f32[1024]{0:T(1024)S(1)}, f32[1024]{0:T(1024)}, u32[]{:S(2)}) copy-start(f32[1024]{0:T(1024)} %param.14) | copy-start | bytes 12292

commit v3 on v2

--- a/solution.py
+++ b/solution.py
@@ -281,12 +281,13 @@
             square = jnp.dot((raw * raw).astype(BF16), ones, preferred_element_type=F32)
             scale = lax.rsqrt(square * (1.0 / DH) + 1e-06)
             out_ref[here, there] = (raw * scale * gain_ref[:, there]).astype(BF16)
+            sem = sems.at[1 + len(copies)]
+            copies.append(pltpu.make_async_copy(out_ref.at[here, there], out_hbm.at[here, there], sem))
+            copies[-1].start()
             if b < tokens // BLK - 1:
                 for one in (h, h + 1):
                     update = first_ref[b, one * DH : (one + 1) * DH, :].astype(F32)
                     state[one] = factor[one : one + 1, :] * state[one] + update
-        copies.append(pltpu.make_async_copy(out_ref.at[here, :], out_hbm.at[here, :], sems.at[1 + b]))
-        copies[b].start()
     soft_copy.wait()
     for copy in copies:
         copy.wait()
@@ -591,7 +592,7 @@
         out_shape=(wide, wide),
         in_specs=[VMEM] * 10,
         out_specs=(HBM, HBM),
-        scratch_shapes=[pltpu.VMEM(lin_q.shape, BF16), pltpu.SemaphoreType.DMA((1 + blocks,))],
+        scratch_shapes=[pltpu.VMEM(lin_q.shape, BF16), pltpu.SemaphoreType.DMA((1 + blocks * heads // 2,))],
         compiler_params=within(12),
         cost_estimate=lasting(3),
         name="across",

time: 26.9 us -> 26.8 us (level)
  transfers between devices with their start and end apart: 5 -> 5, of which waited for: 3 -> 3; matrix products, arithmetic and copies ran while one was open for 0% -> 0% of each run, Pallas kernels for 30% -> 31%
where the time goes in v3:
time: 26.8 us; the launch traced here: 26.6 us
  Pallas kernels  11 us (41%)
  starting transfers between devices  9.22 us (34%)
  waiting for transfers between devices  5.46 us (20%)
  between operations  0.91 us (3%)
    ppermute x5, starting transfers between devices, swapped(): lax.ppermute(value, axis, [(i, i ^ 1 << bit) for i in range(lax.axis_size...  9.22 us
    ppermute x5, waiting for transfers between devices, swapped(): lax.ppermute(value, axis, [(i, i ^ 1 << bit) for i in range(lax.axis_size...  5.46 us
    pallas_call x1, Pallas kernels, local(): pl.pallas_call(states_kernel, out_shape=(pltpu.VMEM(msg.shape, BF16), plt...  2.52 us
    pallas_call x1, Pallas kernels, local(): pl.pallas_call(near_kernel, out_shape=(totals, tops), in_specs=[VMEM, VME...  2.25 us
    pallas_call x1, Pallas kernels, local(): pl.pallas_call(inside_kernel, out_shape=(pltpu.VMEM(lin_q.shape, BF16), p...  2.04 us
    pallas_call x1, Pallas kernels, local(): pl.pallas_call(functools.partial(across_kernel, bits - 1), out_shape=(wid...  1.89 us
    pallas_call x1, Pallas kernels, local(): pl.pallas_call(fetch_kernel, out_shape=(pltpu.VMEM((2 * tokens, DH), BF16...  1.01 us
    pallas_call x1, Pallas kernels, local(): pl.pallas_call(functools.partial(last_kernel, count, late), out_shape=(ja...  0.71 us
  transfers between devices with their start and end apart: 5, of which 3 were waited for; matrix products, arithmetic and copies ran while one was open for 0% of the time, Pallas kernels for 31%

profile of v3, /device:TPU:0, one launch (start us, length us, event | category | flops | bytes accessed | tf_op | source)
XLA Modules:
  0.0 26.6 jit_solution(1916323145977735484)
XLA Ops:
  0.6 1.0 %fetch.1 = (bf16[1024,128]{1,0:T(8,128)(2,1)S(1)}, f32[8,512]{1,0:T(8,128)S(1)}, s32[1,4]{1,0:T(1,128)S(1)}) custom-call(bf16[512,128]{1,0:T(8,128)(2,1)} %keys.1, bf16[512,128]{1,0:T(8,128)(2,1)} %values.1, f32[8,512]{1,0:T(8,128)} %decay.1, s32[1,4]{1,0:T(1,128)} %bitcast.3), custom_call_target="tpu_custom_call" | custom-call | flops 800000000 | tf_op jit(solution)/shard_map/fetch/pallas_call | solution.py:472
  1.6 0.0 copy-start
  1.7 3.0 %collective-permute-start = (bf16[1024,128]{1,0:T(8,128)(2,1)S(1)}, bf16[1024,128]{1,0:T(8,128)(2,1)S(1)}, u32[]{:S(2)}, u32[]{:S(2)}) collective-permute-start(bf16[1024,128]{1,0:T(8,128)(2,1)S(1)} %get-tuple-element.33.own_ref.refs_0_), channel_id=1, source_target_pairs={{0,8},{8,0},{16,24},{24,16},{1,9},{9,1},{17,25},{25,17},{2,10},{10... | collective-permute-start | bytes 786440 | tf_op jit(solution)/shard_map/ppermute | solution.py:39
  4.7 1.5 %collective-permute-start.2 = (bf16[1024,128]{1,0:T(8,128)(2,1)S(1)}, bf16[1024,128]{1,0:T(8,128)(2,1)S(1)}, u32[]{:S(2)}, u32[]{:S(2)}) collective-permute-start(bf16[1024,128]{1,0:T(8,128)(2,1)S(1)} %get-tuple-element.33.own_ref.refs_0_), channel_id=1, source_target_pairs={{0,16},{8,24},{16,0},{24,8},{1,17},{9,25},{17,1},{25,9},{2,18},{10... | collective-permute-start | bytes 786440 | tf_op jit(solution)/shard_map/ppermute | solution.py:39
  6.2 2.5 %states.1 = (bf16[1040,128]{1,0:T(8,128)(2,1)S(1)}, bf16[1,1024,128]{2,1,0:T(8,128)(2,1)S(1)}, f32[8,512]{1,0:T(8,128)S(1)}) custom-call(s32[1,4]{1,0:T(1,128)S(1)} %broadcast_maximum_fusion.lengths_ref, bf16[512,1024]{1,0:T(8,128)(2,1)} %keys_ref, bf16[512,1024]{1,0:T(8,128)(2,1)} %values_ref.1, f32[8,512]{1,0:T(8,128)S(1)} %get-tuple-element.27.decay_ref), custom_call_target="tpu_custom_call" | custom-call | flops 2000000000 | tf_op jit(solution)/shard_map/states/pallas_call | solution.py:496
  8.7 0.0 copy-start.1
  8.7 0.0 copy-start.2
  8.7 0.0 copy-start.3
  8.7 0.6 %collective-permute-start.1 = (bf16[1040,128]{1,0:T(8,128)(2,1)S(1)}, bf16[1040,128]{1,0:T(8,128)(2,1)S(1)}, u32[]{:S(2)}, u32[]{:S(2)}) collective-permute-start(bf16[1040,128]{1,0:T(8,128)(2,1)S(1)} %get-tuple-element.32.total_ref), channel_id=1, source_target_pairs={{0,8},{8,0},{16,24},{24,16},{1,9},{9,1},{17,25},{25,17},{2,10},{10... | collective-permute-start | bytes 798728 | tf_op jit(solution)/shard_map/ppermute | solution.py:39
  9.3 0.0 copy-done
  9.3 2.2 %near.1 = (f32[4096,256]{1,0:T(8,128)S(1)}, f32[4096,128]{1,0:T(8,128)S(1)}) custom-call(s32[1,4]{1,0:T(1,128)S(1)} %broadcast_maximum_fusion.lengths_ref, bf16[512,1024]{1,0:T(8,128)(2,1)S(1)} %copy-done, bf16[1024,128]{1,0:T(8,128)(2,1)S(1)} %get-tuple-element.33.own_ref.refs_0_), custom_call_target="tpu_custom_call" | custom-call | flops 3200000000 | tf_op jit(solution)/shard_map/near/pallas_call | solution.py:547
  11.6 0.0 collective-permute-done.refs_1_
  11.6 2.3 %collective-permute-start.4 = (bf16[1024,128]{1,0:T(8,128)(2,1)S(1)}, bf16[1024,128]{1,0:T(8,128)(2,1)S(1)}, u32[]{:S(2)}, u32[]{:S(2)}) collective-permute-start(bf16[1024,128]{1,0:T(8,128)(2,1)S(1)} %collective-permute-done.refs_1_), channel_id=1, source_target_pairs={{0,16},{8,24},{16,0},{24,8},{1,17},{9,25},{17,1},{25,9},{2,18},{10... | collective-permute-start | bytes 786440 | tf_op jit(solution)/shard_map/ppermute | solution.py:39
  13.9 0.0 copy-done.1
  13.9 0.0 copy-done.2
  13.9 0.0 copy-done.3
  13.9 2.0 %inside.1 = (bf16[512,1024]{1,0:T(8,128)(2,1)S(1)}, f32[512,1024]{1,0:T(8,128)S(1)}) custom-call(s32[1,4]{1,0:T(1,128)S(1)} %broadcast_maximum_fusion.lengths_ref, bf16[512,1024]{1,0:T(8,128)(2,1)S(1)} %copy-done.3, bf16[512,1024]{1,0:T(8,128)(2,1)S(1)} %copy-done.1, bf16[512,1024]{1,0:T(8,128)(2,1)S(1)} %copy-done.2, f32[8,512]{1,0:T(8,128)S(1)} %get-tuple-element.28.sums_ref), custom_call_target="tpu_custom_call" | custom-call | flops 3200000000 | tf_op jit(solution)/shard_map/inside/pallas_call | solution.py:511
  15.9 0.0 collective-permute-done.2.refs_0_.refs_2_
  15.9 0.1 middle.2.totals_in
  16.1 0.6 %collective-permute-done.1.far_ref.prefix_ref = bf16[1040,128]{1,0:T(8,128)(2,1)S(1)} collective-permute-done((bf16[1040,128]{1,0:T(8,128)(2,1)S(1)}, bf16[1040,128]{1,0:T(8,128)(2,1)S(1)}, u32[]{:S(2)}, u32[]{:S(2)}) %collective-permute-start.1) | collective-permute-done | bytes 266272 | tf_op jit(solution)/shard_map/ppermute | solution.py:39
  16.7 0.2 total.1
  16.8 1.8 %collective-permute-start.3 = (bf16[1040,128]{1,0:T(8,128)(2,1)S(1)}, bf16[1040,128]{1,0:T(8,128)(2,1)S(1)}, u32[]{:S(2)}, u32[]{:S(2)}) collective-permute-start(bf16[1040,128]{1,0:T(8,128)(2,1)S(1)} %total.1), channel_id=1, source_target_pairs={{0,16},{8,24},{16,0},{24,8},{1,17},{9,25},{17,1},{25,9},{2,18},{10... | collective-permute-start | bytes 798728 | tf_op jit(solution)/shard_map/ppermute | solution.py:39
  18.7 0.3 %middle.3.totals_in = f32[4096,256]{1,0:T(8,128)S(1)} custom-call(s32[1,4]{1,0:T(1,128)S(1)} %broadcast_maximum_fusion.lengths_ref, bf16[512,1024]{1,0:T(8,128)(2,1)S(1)} %copy-done, f32[4096,128]{1,0:T(8,128)S(1)} %get-tuple-element.34.tops_ref, f32[4096,256]{1,0:T(8,128)S(1)} %middle.2.totals_in, ...), custom_call_target="tpu_custom_call", output_to_operand_aliasing={{}: (3, {})} | custom-call | flops 1600000000 | tf_op jit(solution)/shard_map/middle/pallas_call | solution.py:559
  19.0 0.0 copy-start.4
  19.0 0.2 collective-permute-done.4.refs_3_
  19.2 0.7 %last.1 = (bf16[512,1024]{1,0:T(8,128)(2,1)S(1)}, f32[4096,256]{1,0:T(8,128)S(1)}) custom-call(s32[1,4]{1,0:T(1,128)S(1)} %broadcast_maximum_fusion.lengths_ref, bf16[512,1024]{1,0:T(8,128)(2,1)S(1)} %copy-done, f32[4096,128]{1,0:T(8,128)S(1)} %get-tuple-element.34.tops_ref, f32[4096,256]{1,0:T(8,128)S(1)} %middle.3.totals_in, ...), custom_call_target="tpu_custom_call", output_to_operand_aliasing={{1}: (3, {})} | custom-call | flops 3200000000 | tf_op jit(solution)/shard_map/last/pallas_call | solution.py:578
  19.9 4.7 %collective-permute-done.3.far_ref = bf16[1040,128]{1,0:T(8,128)(2,1)S(1)} collective-permute-done((bf16[1040,128]{1,0:T(8,128)(2,1)S(1)}, bf16[1040,128]{1,0:T(8,128)(2,1)S(1)}, u32[]{:S(2)}, u32[]{:S(2)}) %collective-permute-start.3) | collective-permute-done | bytes 266272 | tf_op jit(solution)/shard_map/ppermute | solution.py:39
  24.6 0.0 copy-done.4
  24.6 1.9 %across.1 = (bf16[512,1024]{1,0:T(8,128)(2,1)}, bf16[512,1024]{1,0:T(8,128)(2,1)}) custom-call(s32[1,4]{1,0:T(1,128)S(1)} %broadcast_maximum_fusion.lengths_ref, bf16[512,1024]{1,0:T(8,128)(2,1)S(1)} %copy-done.3, bf16[512,1024]{1,0:T(8,128)(2,1)S(1)} %get-tuple-element.29.inside_ref, f32[512,1024]{1,0:T(8,128)S(1)} %get-tuple-element.30.entering_ref, ...), custom_call_target="tpu_custom_call" | custom-call | flops 2400000000 | tf_op jit(solution)/shard_map/across/pallas_call | solution.py:590
  (1 shorter events, 0.0 us)
Async XLA Ops:
  1.6 7.7 %copy-start = (bf16[512,1024]{1,0:T(8,128)(2,1)S(1)}, bf16[512,1024]{1,0:T(8,128)(2,1)}, u32[]{:S(2)}) copy-start(bf16[512,1024]{1,0:T(8,128)(2,1)} %queries_ref.9) | copy-start | bytes 3145732
  1.7 9.9 %collective-permute-start = (bf16[1024,128]{1,0:T(8,128)(2,1)S(1)}, bf16[1024,128]{1,0:T(8,128)(2,1)S(1)}, u32[]{:S(2)}, u32[]{:S(2)}) collective-permute-start(bf16[1024,128]{1,0:T(8,128)(2,1)S(1)} %get-tuple-element.33.own_ref.refs_0_), channel_id=1, source_target_pairs={{0,8},{8,0},{16,24},{24,16},{1,9},{9,1},{17,25},{25,17},{2,10},{10... | collective-permute-start | bytes 786440 | tf_op jit(solution)/shard_map/ppermute | solution.py:39
  4.7 11.3 %collective-permute-start.2 = (bf16[1024,128]{1,0:T(8,128)(2,1)S(1)}, bf16[1024,128]{1,0:T(8,128)(2,1)S(1)}, u32[]{:S(2)}, u32[]{:S(2)}) collective-permute-start(bf16[1024,128]{1,0:T(8,128)(2,1)S(1)} %get-tuple-element.33.own_ref.refs_0_), channel_id=1, source_target_pairs={{0,16},{8,24},{16,0},{24,8},{1,17},{9,25},{17,1},{25,9},{2,18},{10... | collective-permute-start | bytes 786440 | tf_op jit(solution)/shard_map/ppermute | solution.py:39
  8.7 5.2 %copy-start.1 = (bf16[512,1024]{1,0:T(8,128)(2,1)S(1)}, bf16[512,1024]{1,0:T(8,128)(2,1)}, u32[]{:S(2)}) copy-start(bf16[512,1024]{1,0:T(8,128)(2,1)} %keys_ref) | copy-start | bytes 3145732
  8.7 5.2 %copy-start.2 = (bf16[512,1024]{1,0:T(8,128)(2,1)S(1)}, bf16[512,1024]{1,0:T(8,128)(2,1)}, u32[]{:S(2)}) copy-start(bf16[512,1024]{1,0:T(8,128)(2,1)} %values_ref.1) | copy-start | bytes 3145732
  8.7 5.2 %copy-start.3 = (bf16[512,1024]{1,0:T(8,128)(2,1)S(1)}, bf16[512,1024]{1,0:T(8,128)(2,1)}, u32[]{:S(2)}) copy-start(bf16[512,1024]{1,0:T(8,128)(2,1)} %queries_ref.10) | copy-start | bytes 3145732
  8.7 7.9 %collective-permute-start.1 = (bf16[1040,128]{1,0:T(8,128)(2,1)S(1)}, bf16[1040,128]{1,0:T(8,128)(2,1)S(1)}, u32[]{:S(2)}, u32[]{:S(2)}) collective-permute-start(bf16[1040,128]{1,0:T(8,128)(2,1)S(1)} %get-tuple-element.32.total_ref), channel_id=1, source_target_pairs={{0,8},{8,0},{16,24},{24,16},{1,9},{9,1},{17,25},{25,17},{2,10},{10... | collective-permute-start | bytes 798728 | tf_op jit(solution)/shard_map/ppermute | solution.py:39
  11.6 7.6 %collective-permute-start.4 = (bf16[1024,128]{1,0:T(8,128)(2,1)S(1)}, bf16[1024,128]{1,0:T(8,128)(2,1)S(1)}, u32[]{:S(2)}, u32[]{:S(2)}) collective-permute-start(bf16[1024,128]{1,0:T(8,128)(2,1)S(1)} %collective-permute-done.refs_1_), channel_id=1, source_target_pairs={{0,16},{8,24},{16,0},{24,8},{1,17},{9,25},{17,1},{25,9},{2,18},{10... | collective-permute-start | bytes 786440 | tf_op jit(solution)/shard_map/ppermute | solution.py:39
  16.8 7.8 %collective-permute-start.3 = (bf16[1040,128]{1,0:T(8,128)(2,1)S(1)}, bf16[1040,128]{1,0:T(8,128)(2,1)S(1)}, u32[]{:S(2)}, u32[]{:S(2)}) collective-permute-start(bf16[1040,128]{1,0:T(8,128)(2,1)S(1)} %total.1), channel_id=1, source_target_pairs={{0,16},{8,24},{16,0},{24,8},{1,17},{9,25},{17,1},{25,9},{2,18},{10... | collective-permute-start | bytes 798728 | tf_op jit(solution)/shard_map/ppermute | solution.py:39
  19.0 5.6 %copy-start.4 = (f32[1024]{0:T(1024)S(1)}, f32[1024]{0:T(1024)}, u32[]{:S(2)}) copy-start(f32[1024]{0:T(1024)} %param.14) | copy-start | bytes 12292
